TPU v7x, 32 devices: a whole 2x2x4 slice. The times are simulated.
32 devices in a mesh: seq: 8 (over y, x, core), exp: 4 (over z).
Axes of the slice: x: 2, y: 2, z: 4, core: 2. Of those that a mesh axis runs over, the one named last changes fastest.
Arguments:
- tokens: bfloat16 [16, 2048, 768], P('exp', 'seq'), may hold values from -6 to 6
- cotangent: bfloat16 [16, 2048, 768], P('exp', 'seq'), may hold values from -6 to 6
- lengths: int32 [4, 4], P('exp'), may hold values from 1 to 2048, 5120 in all within a row
- routes: int32 [16, 2048, 2], P('exp', 'seq'), may hold values from 0 to 7, all different within a row
- gate_weights: float32 [16, 2048, 2], P('exp', 'seq'), may hold values from 0.5 to 1.5
- norm_gains: float32 [768, 2], P(('seq', 'exp'))
- gains_first: float32 [768, 2], P(('seq', 'exp')), may hold values from -160 to 160
- gains_second: float32 [768, 2], P(('seq', 'exp')), may hold values from 49.152 to 196.608
- input_weight: float32 [768, 2304], P(('seq', 'exp'))
- input_first: float32 [768, 2304], P(('seq', 'exp')), may hold values from -80 to 80
- input_second: float32 [768, 2304], P(('seq', 'exp')), may hold values from 17.69472 to 70.77888
- output_weight: float32 [768, 768], P(('seq', 'exp'))
- output_first: float32 [768, 768], P(('seq', 'exp')), may hold values from -40 to 40
- output_second: float32 [768, 768], P(('seq', 'exp')), may hold values from 4.42368 to 17.69472
- frozen_in: bfloat16 [4, 768, 3072], P('exp', 'seq'), may hold values from -0.21875 to 0.21875
- frozen_out: bfloat16 [4, 3072, 768], P('exp', 'seq'), may hold values from -0.109375 to 0.109375
- expert_in: float32 [4, 768, 3072], P('exp', 'seq')
- inner_first: float32 [4, 768, 3072], P('exp', 'seq'), may hold values from -32 to 32
- inner_second: float32 [4, 768, 3072], P('exp', 'seq'), may hold values from 2.21184 to 8.84736
- expert_out: float32 [4, 3072, 768], P('exp', 'seq')
- outer_first: float32 [4, 3072, 768], P('exp', 'seq'), may hold values from -24 to 24
- outer_second: float32 [4, 3072, 768], P('exp', 'seq'), may hold values from 1.10592 to 4.42368
Outputs:
- block_output: bfloat16 [16, 2048, 768], P('exp', 'seq')
- token_grad: float32 [16, 2048, 768], P('exp', 'seq')
- gains_grad: float32 [768, 2], P(('seq', 'exp'))
- gains_moment: float32 [768, 2], P(('seq', 'exp'))
- gains_square: float32 [768, 2], P(('seq', 'exp'))
- gains_new: float32 [768, 2], P(('seq', 'exp'))
- input_grad: float32 [768, 2304], P(('seq', 'exp'))
- input_moment: float32 [768, 2304], P(('seq', 'exp'))
- input_square: float32 [768, 2304], P(('seq', 'exp'))
- input_new: float32 [768, 2304], P(('seq', 'exp'))
- output_grad: float32 [768, 768], P(('seq', 'exp'))
- output_moment: float32 [768, 768], P(('seq', 'exp'))
- output_square: float32 [768, 768], P(('seq', 'exp'))
- output_new: float32 [768, 768], P(('seq', 'exp'))
- inner_grad: float32 [4, 768, 3072], P('exp', 'seq')
- inner_moment: float32 [4, 768, 3072], P('exp', 'seq')
- inner_square: float32 [4, 768, 3072], P('exp', 'seq')
- inner_new: float32 [4, 768, 3072], P('exp', 'seq')
- outer_grad: float32 [4, 3072, 768], P('exp', 'seq')
- outer_moment: float32 [4, 3072, 768], P('exp', 'seq')
- outer_square: float32 [4, 3072, 768], P('exp', 'seq')
- outer_new: float32 [4, 3072, 768], P('exp', 'seq')
- matrix_norms: float32 [12, 2], replicated
- trust_ratios: float32 [12], replicated
- routed_counts: int32 [8], replicated
Inputs may be any that keep to these rules, and one draw needn't show every extreme that they name: `lengths`: each row sums to 5120 and its longest entry is 2048. `routes`: the two experts of a token differ.
All inputs are finite; a program needn't handle non-finite values.
Results may differ from a plain program's by a relative error of at most 0.03.
Values may be sent and summed in bfloat16 or wider, within the bound.
No kernel may reach another device: no remote copies, remote signals or barrier semaphores. Data moves between devices by JAX's collectives and lax.ppermute only.
A program may use at most 320 MiB of HBM per device.

v0:
```python
import jax
import jax.numpy as jnp
from jax import lax
from jax.sharding import PartitionSpec as P

HEADS = 12
HEAD_DIM = 64
STEP = 10


norm_eps = 1e-06
beta_one = 0.9
beta_two = 0.999
lamb_eps = 1e-06
decay_rate = 0.01
learn_rate = 0.3
masked_score = -1e30


def from_behind(block, axis, distance):
    devices = range(lax.axis_size(axis))
    route = [(i - distance, i) for i in devices if i - distance in devices]
    return lax.ppermute(block, axis, route)


def passed_along(block, axis, distance):
    devices = range(lax.axis_size(axis))
    route = [((i - distance) % len(devices), i) for i in devices]
    return lax.ppermute(block, axis, route)


def rms_norm(values, gain):
    factor = lax.rsqrt(jnp.mean(values * values, axis=-1, keepdims=True) + norm_eps)
    return values * factor * gain


def split_heads(values):
    return values.reshape(values.shape[0], values.shape[1], HEADS, HEAD_DIM)


def merge_heads(values):
    return values.reshape(values.shape[0], values.shape[1], HEADS * HEAD_DIM)


def allowed_pairs(query_first, query_count, key_first, key_count, seq_lengths):
    query_pos = query_first + jnp.arange(query_count, dtype=jnp.int32)
    key_pos = key_first + jnp.arange(key_count, dtype=jnp.int32)
    causal = key_pos[None, :] <= query_pos[:, None]
    inside = key_pos[None, None, :] < seq_lengths[:, None, None]
    return (causal[None] & inside)[:, None]


def pair_grads(
    query_block,
    context_grad,
    log_total,
    row_delta,
    query_first,
    key_block,
    value_block,
    key_first,
    seq_lengths,
    longest,
):
    batch_size, query_count, model_width = query_block.shape
    key_count = key_block.shape[1]
    score_scale = HEAD_DIM ** (-0.5)

    def pair_compute(unused):
        allowed = allowed_pairs(query_first, query_count, key_first, key_count, seq_lengths)
        scores = (
            jnp.einsum(
                "sqhd,skhd->shqk",
                split_heads(query_block),
                split_heads(key_block),
                preferred_element_type=jnp.float32,
            )
            * score_scale
        )
        softmax_out = jnp.where(allowed, jnp.exp(scores - log_total[..., None]), 0.0)
        value_grad = jnp.einsum(
            "shqk,sqhd->skhd",
            softmax_out.astype(jnp.bfloat16),
            split_heads(context_grad),
            preferred_element_type=jnp.float32,
        )
        weight_grad = jnp.einsum(
            "sqhd,skhd->shqk",
            split_heads(context_grad),
            split_heads(value_block),
            preferred_element_type=jnp.float32,
        )
        score_grad = (softmax_out * (weight_grad - row_delta[..., None])).astype(jnp.bfloat16)
        query_grad = (
            jnp.einsum(
                "shqk,skhd->sqhd",
                score_grad,
                split_heads(key_block),
                preferred_element_type=jnp.float32,
            )
            * score_scale
        )
        key_grad = (
            jnp.einsum(
                "shqk,sqhd->skhd",
                score_grad,
                split_heads(query_block),
                preferred_element_type=jnp.float32,
            )
            * score_scale
        )
        return (merge_heads(query_grad), merge_heads(key_grad), merge_heads(value_grad))

    def skipped(unused):
        return (
            jnp.zeros((batch_size, query_count, model_width), jnp.float32),
            jnp.zeros((batch_size, key_count, model_width), jnp.float32),
            jnp.zeros((batch_size, key_count, model_width), jnp.float32),
        )

    working = (
        (key_first >= 0) & (key_first <= query_first + query_count - 1) & (key_first < longest)
    )
    return lax.cond(working, pair_compute, skipped, 0)


def lamb_update(weight, grad, first, second, decay):
    first_new = beta_one * first + (1.0 - beta_one) * grad
    second_new = beta_two * second + (1.0 - beta_two) * grad * grad
    update = (
        first_new
        / (1.0 - beta_one**STEP)
        / (jnp.sqrt(second_new / (1.0 - beta_two**STEP)) + lamb_eps)
        + decay * weight
    )
    return (first_new, second_new, update)


def square_pair(weight, update):
    return jnp.stack([jnp.sum(weight * weight), jnp.sum(update * update)])


def body(
    tokens,
    cotangent,
    lengths,
    routes,
    gate_weights,
    norm_gains,
    gains_first,
    gains_second,
    input_weight,
    input_first,
    input_second,
    output_weight,
    output_first,
    output_second,
    frozen_in,
    frozen_out,
    expert_in,
    inner_first,
    inner_second,
    expert_out,
    outer_first,
    outer_second,
):
    seq_devices = lax.axis_size("seq")
    exp_devices = lax.axis_size("exp")
    seq_place = lax.axis_index("seq")
    exp_place = lax.axis_index("exp")
    batch_size, pos_count, model_width = tokens.shape
    tok_count = batch_size * pos_count
    experts = 2 * exp_devices
    capacity = 2 * tok_count // experts
    total_slots = experts * capacity
    first_query = seq_place * pos_count
    seq_lengths = lengths[0]
    longest = jnp.max(seq_lengths)
    score_scale = HEAD_DIM ** (-0.5)
    input_low, output_low, gains_low = (
        lax.all_gather(input_weight.astype(jnp.bfloat16), ("seq", "exp"), axis=0, tiled=True),
        lax.all_gather(output_weight.astype(jnp.bfloat16), ("seq", "exp"), axis=0, tiled=True),
        lax.all_gather(norm_gains.astype(jnp.bfloat16), ("seq", "exp"), axis=0, tiled=True),
    )
    frozen_whole_in, frozen_whole_out, train_whole_in, train_whole_out = (
        lax.all_gather(frozen_in, "seq", axis=1, tiled=True),
        lax.all_gather(frozen_out, "seq", axis=1, tiled=True),
        lax.all_gather(expert_in.astype(jnp.bfloat16), "seq", axis=1, tiled=True),
        lax.all_gather(expert_out.astype(jnp.bfloat16), "seq", axis=1, tiled=True),
    )
    stacked_in = jnp.concatenate([frozen_whole_in, train_whole_in], axis=0)
    stacked_out = jnp.concatenate([frozen_whole_out, train_whole_out], axis=0)
    gain_attend = gains_low[:, 0].astype(jnp.float32)
    gain_expert = gains_low[:, 1].astype(jnp.float32)
    tokens_flat = tokens.reshape(tok_count, model_width).astype(jnp.float32)
    first_normed = rms_norm(tokens_flat, gain_attend).astype(jnp.bfloat16)
    packed = (
        jnp.dot(first_normed, input_low, preferred_element_type=jnp.float32)
        .astype(jnp.bfloat16)
        .reshape(batch_size, pos_count, 3 * model_width)
    )
    query_part = packed[:, :, :model_width]
    key_part = packed[:, :, model_width : 2 * model_width]
    value_part = packed[:, :, 2 * model_width :]
    start_state = (
        jnp.zeros((batch_size, HEADS, pos_count, HEAD_DIM), jnp.float32),
        jnp.full((batch_size, HEADS, pos_count), masked_score, jnp.float32),
        jnp.zeros((batch_size, HEADS, pos_count), jnp.float32),
    )
    key_first = jnp.int32(0)
    key_block = lax.all_gather(key_part, "seq", axis=1, tiled=True)
    value_block = lax.all_gather(value_part, "seq", axis=1, tiled=True)
    key_count = key_block.shape[1]

    def fold_compute(state):
        weighted, run_peak, run_total = state
        allowed = allowed_pairs(first_query, pos_count, key_first, key_count, seq_lengths)
        scores = (
            jnp.einsum(
                "sqhd,skhd->shqk",
                split_heads(query_part),
                split_heads(key_block),
                preferred_element_type=jnp.float32,
            )
            * score_scale
        )
        masked = jnp.where(allowed, scores, masked_score)
        new_peak = jnp.maximum(run_peak, jnp.max(masked, axis=-1))
        shifted = jnp.where(allowed, jnp.exp(masked - new_peak[..., None]), 0.0)
        new_total = jnp.sum(shifted, axis=-1)
        new_weighted = jnp.einsum(
            "shqk,skhd->shqd",
            shifted.astype(jnp.bfloat16),
            split_heads(value_block),
            preferred_element_type=jnp.float32,
        )
        return (new_weighted, new_peak, new_total)

    def unchanged(state):
        return state

    working = (key_first <= first_query + pos_count - 1) & (key_first < longest)
    weighted, run_peak, run_total = lax.cond(working, fold_compute, unchanged, start_state)
    log_total = run_peak + jnp.log(run_total)
    context = (
        jnp.transpose(weighted / run_total[..., None], (0, 2, 1, 3))
        .reshape(batch_size, pos_count, model_width)
        .astype(jnp.bfloat16)
    )
    context_flat = context.reshape(tok_count, model_width)
    middle = tokens_flat + jnp.dot(context_flat, output_low, preferred_element_type=jnp.float32)
    second_normed = rms_norm(middle, gain_expert).astype(jnp.bfloat16)
    query_positions = first_query + jnp.arange(pos_count, dtype=jnp.int32)
    live_tokens = (query_positions[None, :] < seq_lengths[:, None]).reshape(tok_count)
    pair_routes = routes.reshape(tok_count * 2)
    pair_live = jnp.repeat(live_tokens, 2)
    expert_hits = (
        pair_routes[:, None] == jnp.arange(experts, dtype=jnp.int32)[None, :]
    ) & pair_live[:, None]
    running = jnp.cumsum(expert_hits.astype(jnp.int32), axis=0) - 1
    pair_rank = jnp.sum(jnp.where(expert_hits, running, 0), axis=1)
    pair_kept = pair_live & (pair_rank < capacity)
    pair_slot = jnp.where(pair_kept, pair_routes * capacity + pair_rank, 0)
    slot_owner = (
        jnp.full((total_slots,), -1, jnp.int32)
        .at[jnp.where(pair_kept, pair_slot, total_slots)]
        .set(jnp.arange(tok_count * 2, dtype=jnp.int32), mode="drop")
    )
    slot_filled = slot_owner >= 0
    owner_pair = jnp.maximum(slot_owner, 0)
    counts_local = jnp.sum((expert_hits & pair_kept[:, None]).astype(jnp.float32), axis=0)
    dispatch = jnp.where(
        slot_filled[:, None], jnp.take(second_normed, owner_pair // 2, axis=0), 0
    ).reshape(experts, capacity, model_width)
    pair_gate = jnp.where(pair_kept, gate_weights.reshape(tok_count * 2), 0.0)

    def expert_hidden(received):
        groups = received.reshape(exp_devices, 2, received.shape[1], model_width)
        return jnp.einsum("gjcd,jdf->gjcf", groups, stacked_in, preferred_element_type=jnp.float32)

    hidden = expert_hidden(lax.all_to_all(dispatch, "exp", split_axis=0, concat_axis=0, tiled=True))
    activated = jax.nn.gelu(hidden).astype(jnp.bfloat16)
    result_rows = jnp.einsum(
        "gjcf,jfd->gjcd", activated, stacked_out, preferred_element_type=jnp.float32
    ).astype(jnp.bfloat16)
    returned = lax.all_to_all(
        result_rows.reshape(exp_devices * 2, hidden.shape[2], model_width),
        "exp",
        split_axis=0,
        concat_axis=0,
        tiled=True,
    )
    picked = (
        jnp.take(returned.reshape(total_slots, model_width), pair_slot, axis=0).astype(jnp.float32)
        * pair_gate[:, None]
    )
    mixture = jnp.sum(picked.reshape(tok_count, 2, model_width), axis=1)
    block_output = (
        (middle + mixture).astype(jnp.bfloat16).reshape(batch_size, pos_count, model_width)
    )
    grad_rows = cotangent.reshape(tok_count, model_width).astype(jnp.float32)
    pair_grad = (jnp.repeat(grad_rows, 2, axis=0) * pair_gate[:, None]).astype(jnp.bfloat16)
    grad_dispatch = jnp.where(
        slot_filled[:, None], jnp.take(pair_grad, owner_pair, axis=0), 0
    ).reshape(experts, capacity, model_width)
    received_tokens, received_grads = (
        lax.all_to_all(dispatch, "exp", split_axis=0, concat_axis=0, tiled=True),
        lax.all_to_all(grad_dispatch, "exp", split_axis=0, concat_axis=0, tiled=True),
    )
    hidden_back = expert_hidden(received_tokens)
    token_groups = received_tokens.reshape(exp_devices, 2, capacity, model_width)
    grad_groups = received_grads.reshape(exp_devices, 2, capacity, model_width)
    activated, gelu_back = jax.vjp(jax.nn.gelu, hidden_back)
    active_grad = jnp.einsum(
        "gjcd,jfd->gjcf", grad_groups, stacked_out, preferred_element_type=jnp.float32
    )
    hidden_grad = gelu_back(active_grad)[0].astype(jnp.bfloat16)
    inner_local = jnp.einsum(
        "gcd,gcf->df", token_groups[:, 1], hidden_grad[:, 1], preferred_element_type=jnp.float32
    )[None]
    outer_local = jnp.einsum(
        "gcf,gcd->fd",
        activated[:, 1].astype(jnp.bfloat16),
        grad_groups[:, 1],
        preferred_element_type=jnp.float32,
    )[None]
    copy_grad = (
        jnp.einsum("gjcf,jdf->gjcd", hidden_grad, stacked_in, preferred_element_type=jnp.float32)
        .astype(jnp.bfloat16)
        .reshape(exp_devices * 2, capacity, model_width)
    )
    returned_grad = lax.all_to_all(copy_grad, "exp", split_axis=0, concat_axis=0, tiled=True)
    back_rows = jnp.take(returned_grad.reshape(total_slots, model_width), pair_slot, axis=0).astype(
        jnp.float32
    )
    second_grad = jnp.sum(
        jnp.where(pair_kept[:, None], back_rows, 0.0).reshape(tok_count, 2, model_width), axis=1
    )
    middle_part, gain_expert_grad = jax.vjp(rms_norm, middle, gain_expert)[1](second_grad)
    middle_grad = grad_rows + middle_part
    branch_grad = middle_grad.astype(jnp.bfloat16)
    output_local = jnp.einsum(
        "td,te->de", context_flat, branch_grad, preferred_element_type=jnp.float32
    )
    context_grad = (
        jnp.einsum("te,de->td", branch_grad, output_low, preferred_element_type=jnp.float32)
        .astype(jnp.bfloat16)
        .reshape(batch_size, pos_count, model_width)
    )
    row_delta = jnp.transpose(
        jnp.sum(
            split_heads(context_grad.astype(jnp.float32))
            * split_heads(context.astype(jnp.float32)),
            axis=-1,
        ),
        (0, 2, 1),
    )
    zero_block = jnp.zeros((batch_size, pos_count, model_width), jnp.float32)

    def key_turn(turn_index, state):
        key_block, value_block, key_grad_run, value_grad_run, query_grad_run = state
        owner_index = seq_place - turn_index
        query_add, key_add, value_add = pair_grads(
            query_part,
            context_grad,
            log_total,
            row_delta,
            first_query,
            key_block,
            value_block,
            owner_index * pos_count,
            seq_lengths,
            longest,
        )
        key_block, value_block = from_behind((key_block, value_block), "seq", 1)
        key_grad_run, value_grad_run = (
            passed_along((key_grad_run + key_add).astype(jnp.bfloat16), "seq", 1).astype(
                jnp.float32
            ),
            passed_along((value_grad_run + value_add).astype(jnp.bfloat16), "seq", 1).astype(
                jnp.float32
            ),
        )
        return (key_block, value_block, key_grad_run, value_grad_run, query_grad_run + query_add)

    ended = lax.fori_loop(
        0, seq_devices, key_turn, (key_part, value_part, zero_block, zero_block, zero_block)
    )
    key_grad, value_grad, query_grad = (ended[2], ended[3], ended[4])
    packed_grad = (
        jnp.concatenate([query_grad, key_grad, value_grad], axis=-1)
        .astype(jnp.bfloat16)
        .reshape(tok_count, 3 * model_width)
    )
    input_local = jnp.einsum(
        "td,te->de", first_normed, packed_grad, preferred_element_type=jnp.float32
    )
    first_grad = jnp.einsum("te,de->td", packed_grad, input_low, preferred_element_type=jnp.float32)
    token_part, gain_attend_grad = jax.vjp(rms_norm, tokens_flat, gain_attend)[1](first_grad)
    token_grad = (middle_grad + token_part).reshape(batch_size, pos_count, model_width)
    gains_local = jnp.stack([gain_attend_grad, gain_expert_grad], axis=1)
    input_grad, output_grad, gains_grad = (
        lax.psum_scatter(input_local, ("seq", "exp"), scatter_dimension=0, tiled=True),
        lax.psum_scatter(output_local, ("seq", "exp"), scatter_dimension=0, tiled=True),
        lax.psum_scatter(gains_local, ("seq", "exp"), scatter_dimension=0, tiled=True),
    )
    inner_grad, outer_grad = (
        lax.psum_scatter(
            inner_local.astype(jnp.bfloat16), "seq", scatter_dimension=1, tiled=True
        ).astype(jnp.float32),
        lax.psum_scatter(
            outer_local.astype(jnp.bfloat16), "seq", scatter_dimension=1, tiled=True
        ).astype(jnp.float32),
    )
    gains_moment, gains_square, gains_update = lamb_update(
        norm_gains, gains_grad, gains_first, gains_second, 0.0
    )
    input_moment, input_square, input_update = lamb_update(
        input_weight, input_grad, input_first, input_second, decay_rate
    )
    output_moment, output_square, output_update = lamb_update(
        output_weight, output_grad, output_first, output_second, decay_rate
    )
    inner_moment, inner_square, inner_update = lamb_update(
        expert_in, inner_grad, inner_first, inner_second, decay_rate
    )
    outer_moment, outer_square, outer_update = lamb_update(
        expert_out, outer_grad, outer_first, outer_second, decay_rate
    )
    picker = (jnp.arange(exp_devices, dtype=jnp.int32) == exp_place).astype(jnp.float32)[:, None]
    gains_rows = jnp.stack(
        [jnp.sum(norm_gains * norm_gains, axis=0), jnp.sum(gains_update * gains_update, axis=0)],
        axis=1,
    )
    squares_local = jnp.concatenate(
        [
            square_pair(input_weight, input_update)[None],
            square_pair(output_weight, output_update)[None],
            gains_rows,
            picker * square_pair(expert_in, inner_update)[None],
            picker * square_pair(expert_out, outer_update)[None],
        ],
        axis=0,
    )
    squares_all, counts_all = lax.psum((squares_local, counts_local), ("seq", "exp"))
    matrix_norms = jnp.sqrt(squares_all)
    trust_ratios = matrix_norms[:, 0] / matrix_norms[:, 1]
    input_new = input_weight - learn_rate * trust_ratios[0] * input_update
    output_new = output_weight - learn_rate * trust_ratios[1] * output_update
    gains_new = norm_gains - learn_rate * trust_ratios[2:4][None, :] * gains_update
    inner_trust = lax.dynamic_index_in_dim(trust_ratios, 4 + exp_place, keepdims=False)
    outer_trust = lax.dynamic_index_in_dim(
        trust_ratios, 4 + exp_devices + exp_place, keepdims=False
    )
    inner_new = expert_in - learn_rate * inner_trust * inner_update
    outer_new = expert_out - learn_rate * outer_trust * outer_update
    routed_counts = counts_all.astype(jnp.int32)
    return (
        block_output,
        token_grad,
        gains_grad,
        gains_moment,
        gains_square,
        gains_new,
        input_grad,
        input_moment,
        input_square,
        input_new,
        output_grad,
        output_moment,
        output_square,
        output_new,
        inner_grad,
        inner_moment,
        inner_square,
        inner_new,
        outer_grad,
        outer_moment,
        outer_square,
        outer_new,
        matrix_norms,
        trust_ratios,
        routed_counts,
    )


def solution(mesh):
    return jax.shard_map(
        body,
        mesh=mesh,
        in_specs=(
            P("exp", "seq", None),
            P("exp", "seq", None),
            P("exp", None),
            P("exp", "seq", None),
            P("exp", "seq", None),
            P(("seq", "exp"), None),
            P(("seq", "exp"), None),
            P(("seq", "exp"), None),
            P(("seq", "exp"), None),
            P(("seq", "exp"), None),
            P(("seq", "exp"), None),
            P(("seq", "exp"), None),
            P(("seq", "exp"), None),
            P(("seq", "exp"), None),
            P("exp", "seq", None),
            P("exp", "seq", None),
            P("exp", "seq", None),
            P("exp", "seq", None),
            P("exp", "seq", None),
            P("exp", "seq", None),
            P("exp", "seq", None),
            P("exp", "seq", None),
        ),
        out_specs=(
            P("exp", "seq", None),
            P("exp", "seq", None),
            P(("seq", "exp"), None),
            P(("seq", "exp"), None),
            P(("seq", "exp"), None),
            P(("seq", "exp"), None),
            P(("seq", "exp"), None),
            P(("seq", "exp"), None),
            P(("seq", "exp"), None),
            P(("seq", "exp"), None),
            P(("seq", "exp"), None),
            P(("seq", "exp"), None),
            P(("seq", "exp"), None),
            P(("seq", "exp"), None),
            P("exp", "seq", None),
            P("exp", "seq", None),
            P("exp", "seq", None),
            P("exp", "seq", None),
            P("exp", "seq", None),
            P("exp", "seq", None),
            P("exp", "seq", None),
            P("exp", "seq", None),
            P(),
            P(),
            P(),
        ),
        check_vma=False,
    )
```

profile of v0, /device:TPU:0, one launch (start us, length us, event | category | flops | bytes accessed | tf_op | source)
XLA Modules:
  0.0 1935.7 jit_solution(14249536655272206571)
XLA Ops:
  10.4 69.4 %all-gather = bf16[32,24,2]{1,2,0:T(2,128)(2,1)S(1)} all-gather(bf16[1,24,2]{1,2,0:T(2,128)(2,1)S(1)} %get-tuple-element.585), channel_id=1, replica_groups=mesh['seq'=8,'exp'=4] {'seq','exp'}, dimensions={0}, use_global_device_ids=true | all-gather | bytes 3168 | tf_op jit(solution)/shard_map/all_gather | solution.py:183
  120.3 44.3 %all-gather.12.cloned.1.call-done = bf16[4,2048,768]{1,2,0:T(8,128)(2,1)} async-done(((bf16[4,256,768]{1,2,0:T(8,128)(2,1)}), bf16[4,2048,768]{1,2,0:T(8,128)(2,1)}) %all-gather.12.cloned.1.call-update) | async-done | bytes 12582928 | tf_op jit(solution)/shard_map/all_gather | solution.py:211
  164.7 76.5 %all-gather.14.cloned.1.call-done = bf16[4,2048,768]{1,2,0:T(8,128)(2,1)} async-done(((bf16[4,256,768]{1,2,0:T(8,128)(2,1)}), bf16[4,2048,768]{1,2,0:T(8,128)(2,1)}) %all-gather.14.cloned.1.call-update) | async-done | bytes 12582928 | tf_op jit(solution)/shard_map/all_gather | solution.py:212
  241.1 120.3 %conditional.2 = (f32[4,12,256]{2,1,0:T(8,128)S(1)}, f32[4,12,256]{2,1,0:T(8,128)}, f32[4,12,256]{2,1,0:T(8,128)}, f32[4,12,256,64]{2,0,3,1:T(4,128)}) conditional(s32[]{:T(128)} %convert_element_type.223, () %tuple.48, (s32[]{:T(128)}, s32[1,4]{1,0:T(1,128)S(1)}, bf16[4,256,768]{1,2,0:T(8,128)(2,1)}, bf16[4,2048,768]{1,2,0:T(8,128)(2,1)}, ...), branch_computations={%region_2.0_spmd, %region_3.6_spmd} | conditional | flops 6772224000 | bytes 348407904 | solution.py:243
  243.1 39.4 %fusion = (f32[4,12,256]{2,1,0:T(8,128)S(1)}, f32[4,12,256,2048]{3,2,1,0:T(8,128)}) fusion(pred[4,256,2048]{2,1,0:T(8,128)(4,1)S(1)} %broadcast_and_fusion, bf16[4,256,12,64]{1,3,2,0:T(8,128)(2,1)} %bitcast.1, bf16[4,2048,12,64]{1,3,2,0:T(8,128)(2,1)} %bitcast.231), kind=kOutput, calls=%fused_computation.7 | convolution fusion | flops 3296710656 | bytes 116965376 | tf_op jit(solution)/shard_map/cond/branch_1_fun/sqhd,skhd->shqk/dot_general | solution.py:219
  282.5 33.2 %fusion.1 = f32[4,12,256]{2,1,0:T(8,128)} fusion(f32[4,12,256,2048]{3,2,1,0:T(8,128)} %get-tuple-element.569, f32[4,12,256]{2,1,0:T(8,128)S(1)} %broadcast_maximum_fusion, pred[4,256,2048]{2,1,0:T(8,128)(4,1)S(1)} %broadcast_and_fusion), kind=kLoop, calls=%fused_computation.8 | loop fusion | flops 125816832 | bytes 102858752 | tf_op jit(solution)/shard_map/cond/branch_1_fun/reduce_sum | solution.py:230
  317.2 40.1 %fusion.3 = f32[4,12,256,64]{2,3,1,0:T(8,128)S(1)} fusion(bf16[4,2048,12,64]{1,3,2,0:T(8,128)(2,1)} %bitcast.265, f32[4,12,256,2048]{3,2,1,0:T(8,128)} %get-tuple-element.569, f32[4,12,256]{2,1,0:T(8,128)S(1)} %broadcast_maximum_fusion, pred[4,256,2048]{2,1,0:T(8,128)(4,1)S(1)} %broadcast_and_fusion), kind=kOutput, calls=%fused_computation.10 | convolution fusion | flops 3347054592 | bytes 118538240 | tf_op jit(solution)/shard_map/cond/branch_1_fun/shqk,skhd->shqd/dot_general | solution.py:231
  371.5 9.5 gather_fusion
  402.5 57.8 %all-to-all-done = bf16[8,256,768]{2,1,0:T(8,128)(2,1)S(1)} async-done(((bf16[8,256,768]{2,1,0:T(8,128)(2,1)}), bf16[8,256,768]{2,1,0:T(8,128)(2,1)S(1)}, u32[]{:S(2)}, u32[]{:S(2)}) %all-to-all-start) | async-done | bytes 3145760 | tf_op jit(solution)/shard_map/all_to_all | solution.py:281
  460.4 22.2 %fusion.32 = (bf16[4,2,256,3072]{2,3,0,1:T(8,128)(2,1)}, f32[2,3072,4,256]{3,1,2,0:T(8,128)}) fusion(bf16[4,2,256,768]{3,2,1,0:T(8,128)(2,1)S(1)} %bitcast.238, bf16[1,768,3072]{1,2,0:T(8,128)(2,1)} %copy.151, bf16[1,768,3072]{1,2,0:T(8,128)(2,1)} %copy.150), kind=kOutput, calls=%fused_computation.59 | convolution fusion | flops 9739173888 | bytes 50331648 | tf_op jit(solution)/shard_map/gjcd,jdf->gjcf/dot_general | solution.py:279
  482.6 15.7 convert_bitcast_fusion.1
  522.3 53.1 %all-to-all-done.1 = bf16[8,256,768]{2,1,0:T(8,128)(2,1)S(1)} async-done(((bf16[8,256,768]{2,1,0:T(8,128)(2,1)}), bf16[8,256,768]{2,1,0:T(8,128)(2,1)S(1)}, u32[]{:S(2)}, u32[]{:S(2)}) %all-to-all-start.1) | async-done | bytes 3145760 | tf_op jit(solution)/shard_map/all_to_all | solution.py:286
  575.4 9.4 gather_fusion.1
  590.8 9.4 gather_fusion.2
  602.4 72.7 %all_to_all.21 = bf16[8,256,768]{2,1,0:T(8,128)(2,1)S(1)} all-to-all(bf16[8,256,768]{2,1,0:T(8,128)(2,1)S(1)} %bitcast.234), channel_id=1, replica_groups=mesh['seq'=8,'exp'=4] {'exp'}, dimensions={0} | all-to-all | bytes 6291456 | tf_op jit(solution)/shard_map/all_to_all | solution.py:308
  675.1 11.1 fusion.39
  686.3 30.6 %fusion.28 = bf16[4,2,256,3072]{2,3,0,1:T(8,128)(2,1)} fusion(f32[2,3072,4,256]{3,1,2,0:T(8,128)} %get-tuple-element.595, bf16[1,3072,768]{1,2,0:T(8,128)(2,1)} %all-gather.20.cloned.1.call-done, bf16[1,3072,768]{1,2,0:T(8,128)(2,1)} %all-gather.18.cloned.1.call-done, bf16[4,2,256,768]{3,2,1,0:T(8,128)(2,1)S(1)} %bitcast.241), kind=kOutput, calls=%fused_computation.52 | convolution fusion | flops 9808379904 | bytes 50331648 | tf_op jit(solution)/shard_map/gjcd,jfd->gjcf/dot_general | solution.py:314
  716.9 16.1 convert_bitcast_fusion
  739.6 9.1 fusion.38
  750.5 8.9 reshape.512
  759.4 12.6 reduce_sum.228
  772.0 37.0 %all-to-all-done.3 = bf16[8,256,768]{2,1,0:T(8,128)(2,1)S(1)} async-done(((bf16[8,256,768]{2,1,0:T(8,128)(2,1)}), bf16[8,256,768]{2,1,0:T(8,128)(2,1)S(1)}, u32[]{:S(2)}, u32[]{:S(2)}) %all-to-all-start.3) | async-done | bytes 3145760 | tf_op jit(solution)/shard_map/all_to_all | solution.py:332
  809.0 9.5 gather_fusion.3
  831.4 12.0 reduce_sum.229
  867.4 803.2 %while.24 = (s32[]{:T(128)}, bf16[4,256,768]{1,2,0:T(8,128)(2,1)S(1)}, bf16[4,256,768]{1,2,0:T(8,128)(2,1)}, f32[4,256,768]{1,2,0:T(8,128)}, f32[4,256,768]{1,2,...) while((s32[]{:T(128)}, ...), condition=%wide.region_18.20_spmd.clone, body=%wide.region_15.19_spmd.clone.sunk | while | flops 2054489600 | bytes 210263712 | solution.py:386
  871.0 32.6 %conditional.5 = (f32[4,256,768]{1,2,0:T(8,128)}, f32[4,256,768]{1,2,0:T(8,128)}, f32[4,256,768]{1,2,0:T(8,128)}) conditional(s32[]{:T(128)} %convert_element_type.351, () %tuple.113, (s32[]{:T(128)}, s32[]{:T(128)}, s32[1,4]{1,0:T(1,128)S(1)}, bf16[4,256,768]{1,2,0:T(8,128)(2,1)}, bf16[4,256,768]{1,2,0:T(8,128)(2,1)S(1)}, ...), branch_computations={%region_16.17_spmd, %region_17.18_spmd} | conditional | flops 2046625280 | bytes 125328528 | solution.py:124
  881.5 9.7 multiply_convert_fusion
  921.3 11.2 collective-permute-done.2
  935.8 14.7 collective-permute-done.3
  967.9 55.0 %collective-permute-start.2 = (bf16[4,256,768]{1,2,0:T(8,128)(2,1)}, bf16[4,256,768]{1,2,0:T(8,128)(2,1)}, u32[]{:S(2)}, u32[]{:S(2)}) collective-permute-start(bf16[4,256,768]{1,2,0:T(8,128)(2,1)} %fusion.112), channel_id=1, source_target_pairs={{28,0},{0,4},{4,8},{8,12},{12,16},{16,20},{20,24},{24,28},{29,1},{... | collective-permute-start | bytes 4718600 | tf_op jit(solution)/shard_map/while/body/eval_jaxpr/ppermute | solution.py:29
  1064.8 42.8 %collective-permute-start.2 = (bf16[4,256,768]{1,2,0:T(8,128)(2,1)}, bf16[4,256,768]{1,2,0:T(8,128)(2,1)}, u32[]{:S(2)}, u32[]{:S(2)}) collective-permute-start(bf16[4,256,768]{1,2,0:T(8,128)(2,1)} %fusion.112), channel_id=1, source_target_pairs={{28,0},{0,4},{4,8},{8,12},{12,16},{16,20},{20,24},{24,28},{29,1},{... | collective-permute-start | bytes 4718600 | tf_op jit(solution)/shard_map/while/body/eval_jaxpr/ppermute | solution.py:29
  1111.1 29.0 %collective-permute-start.3 = (bf16[4,256,768]{1,2,0:T(8,128)(2,1)}, bf16[4,256,768]{1,2,0:T(8,128)(2,1)}, u32[]{:S(2)}, u32[]{:S(2)}) collective-permute-start(bf16[4,256,768]{1,2,0:T(8,128)(2,1)} %fusion.113), channel_id=1, source_target_pairs={{28,0},{0,4},{4,8},{8,12},{12,16},{16,20},{20,24},{24,28},{29,1},{... | collective-permute-start | bytes 4718600 | tf_op jit(solution)/shard_map/while/body/eval_jaxpr/ppermute | solution.py:29
  1172.0 46.9 %collective-permute-start.2 = (bf16[4,256,768]{1,2,0:T(8,128)(2,1)}, bf16[4,256,768]{1,2,0:T(8,128)(2,1)}, u32[]{:S(2)}, u32[]{:S(2)}) collective-permute-start(bf16[4,256,768]{1,2,0:T(8,128)(2,1)} %fusion.112), channel_id=1, source_target_pairs={{28,0},{0,4},{4,8},{8,12},{12,16},{16,20},{20,24},{24,28},{29,1},{... | collective-permute-start | bytes 4718600 | tf_op jit(solution)/shard_map/while/body/eval_jaxpr/ppermute | solution.py:29
  1224.8 27.3 %collective-permute-start = (bf16[4,256,768]{1,2,0:T(8,128)(2,1)S(1)}, bf16[4,256,768]{1,2,0:T(8,128)(2,1)S(1)}, u32[]{:S(2)}, u32[]{:S(2)}) collective-permute-start(bf16[4,256,768]{1,2,0:T(8,128)(2,1)S(1)} %copy.230), channel_id=1, source_target_pairs={{0,4},{4,8},{8,12},{12,16},{16,20},{20,24},{24,28},{1,5},{5,9},{9,... | collective-permute-start | bytes 4718600 | tf_op jit(solution)/shard_map/while/body/eval_jaxpr/ppermute | solution.py:23
  1284.1 31.4 %collective-permute-start.2 = (bf16[4,256,768]{1,2,0:T(8,128)(2,1)}, bf16[4,256,768]{1,2,0:T(8,128)(2,1)}, u32[]{:S(2)}, u32[]{:S(2)}) collective-permute-start(bf16[4,256,768]{1,2,0:T(8,128)(2,1)} %fusion.112), channel_id=1, source_target_pairs={{28,0},{0,4},{4,8},{8,12},{12,16},{16,20},{20,24},{24,28},{29,1},{... | collective-permute-start | bytes 4718600 | tf_op jit(solution)/shard_map/while/body/eval_jaxpr/ppermute | solution.py:29
  1321.5 16.2 collective-permute-start
  1337.8 32.9 %collective-permute-start.1 = (bf16[4,256,768]{1,2,0:T(8,128)(2,1)}, bf16[4,256,768]{1,2,0:T(8,128)(2,1)}, u32[]{:S(2)}, u32[]{:S(2)}) collective-permute-start(bf16[4,256,768]{1,2,0:T(8,128)(2,1)} %copy.231), channel_id=1, source_target_pairs={{0,4},{4,8},{8,12},{12,16},{16,20},{20,24},{24,28},{1,5},{5,9},{9,... | collective-permute-start | bytes 4718600 | tf_op jit(solution)/shard_map/while/body/eval_jaxpr/ppermute | solution.py:23
  1396.2 19.6 %collective-permute-start.2 = (bf16[4,256,768]{1,2,0:T(8,128)(2,1)}, bf16[4,256,768]{1,2,0:T(8,128)(2,1)}, u32[]{:S(2)}, u32[]{:S(2)}) collective-permute-start(bf16[4,256,768]{1,2,0:T(8,128)(2,1)} %fusion.112), channel_id=1, source_target_pairs={{28,0},{0,4},{4,8},{8,12},{12,16},{16,20},{20,24},{24,28},{29,1},{... | collective-permute-start | bytes 4718600 | tf_op jit(solution)/shard_map/while/body/eval_jaxpr/ppermute | solution.py:29
  1421.8 28.0 %collective-permute-start = (bf16[4,256,768]{1,2,0:T(8,128)(2,1)S(1)}, bf16[4,256,768]{1,2,0:T(8,128)(2,1)S(1)}, u32[]{:S(2)}, u32[]{:S(2)}) collective-permute-start(bf16[4,256,768]{1,2,0:T(8,128)(2,1)S(1)} %copy.230), channel_id=1, source_target_pairs={{0,4},{4,8},{8,12},{12,16},{16,20},{20,24},{24,28},{1,5},{5,9},{9,... | collective-permute-start | bytes 4718600 | tf_op jit(solution)/shard_map/while/body/eval_jaxpr/ppermute | solution.py:23
  1481.8 31.4 %collective-permute-start.2 = (bf16[4,256,768]{1,2,0:T(8,128)(2,1)}, bf16[4,256,768]{1,2,0:T(8,128)(2,1)}, u32[]{:S(2)}, u32[]{:S(2)}) collective-permute-start(bf16[4,256,768]{1,2,0:T(8,128)(2,1)} %fusion.112), channel_id=1, source_target_pairs={{28,0},{0,4},{4,8},{8,12},{12,16},{16,20},{20,24},{24,28},{29,1},{... | collective-permute-start | bytes 4718600 | tf_op jit(solution)/shard_map/while/body/eval_jaxpr/ppermute | solution.py:29
  1519.2 23.9 %collective-permute-start = (bf16[4,256,768]{1,2,0:T(8,128)(2,1)S(1)}, bf16[4,256,768]{1,2,0:T(8,128)(2,1)S(1)}, u32[]{:S(2)}, u32[]{:S(2)}) collective-permute-start(bf16[4,256,768]{1,2,0:T(8,128)(2,1)S(1)} %copy.230), channel_id=1, source_target_pairs={{0,4},{4,8},{8,12},{12,16},{16,20},{20,24},{24,28},{1,5},{5,9},{9,... | collective-permute-start | bytes 4718600 | tf_op jit(solution)/shard_map/while/body/eval_jaxpr/ppermute | solution.py:23
  1575.1 31.4 %collective-permute-start.2 = (bf16[4,256,768]{1,2,0:T(8,128)(2,1)}, bf16[4,256,768]{1,2,0:T(8,128)(2,1)}, u32[]{:S(2)}, u32[]{:S(2)}) collective-permute-start(bf16[4,256,768]{1,2,0:T(8,128)(2,1)} %fusion.112), channel_id=1, source_target_pairs={{28,0},{0,4},{4,8},{8,12},{12,16},{16,20},{20,24},{24,28},{29,1},{... | collective-permute-start | bytes 4718600 | tf_op jit(solution)/shard_map/while/body/eval_jaxpr/ppermute | solution.py:29
  1610.0 8.9 collective-permute-start.3
  1618.9 22.7 %collective-permute-start = (bf16[4,256,768]{1,2,0:T(8,128)(2,1)S(1)}, bf16[4,256,768]{1,2,0:T(8,128)(2,1)S(1)}, u32[]{:S(2)}, u32[]{:S(2)}) collective-permute-start(bf16[4,256,768]{1,2,0:T(8,128)(2,1)S(1)} %copy.230), channel_id=1, source_target_pairs={{0,4},{4,8},{8,12},{12,16},{16,20},{20,24},{24,28},{1,5},{5,9},{9,... | collective-permute-start | bytes 4718600 | tf_op jit(solution)/shard_map/while/body/eval_jaxpr/ppermute | solution.py:23
  1656.3 11.0 collective-permute-done.3
  1697.4 100.4 %all-reduce = f32[768,2]{0,1:T(2,128)S(1)} all-reduce(f32[768,2]{0,1:T(2,128)S(1)} %pad_maximum_fusion.3), channel_id=2, replica_groups=mesh['seq'=8,'exp'=4] {'seq','exp'}, use_global_device_ids=true, to_apply=%region_22.24.clone | all-reduce | flops 1536 | bytes 12288
  1814.5 53.9 %reduce-scatter.6.cloned.1.call-done = f32[24,2304]{1,0:T(8,128)} async-done(((f32[768,2304]{1,0:T(8,128)}), f32[24,2304]{1,0:T(8,128)}) %reduce-scatter.6.cloned.1.call-update) | async-done | bytes 221200 | tf_op jit(solution)/shard_map/reduce_scatter | solution.py:403
  1877.2 40.0 %all-reduce.1 = (f32[12,2]{0,1:T(2,128)S(1)}, f32[8]{0:T(128)S(1)}) all-reduce(f32[12,2]{0,1:T(2,128)S(1)} %concatenate.26, f32[8]{0:T(128)S(1)} %convert_reduce_fusion), channel_id=1, replica_groups=mesh['seq'=8,'exp'=4] {'seq','exp'}, use_global_device_ids=true, to_apply=%region_37.39 | all-reduce | flops 32 | bytes 256 | tf_op jit(solution)/shard_map/psum | solution.py:445
  (510 shorter events, 562.9 us)
Async XLA Ops:
  7.2 76.3 %all-gather.10.cloned.1.call-start = ((), (), s32[]{:S(2)}) async-start(), calls=%async_computation.8 | async-start | bytes 3649536 | tf_op jit(solution)/shard_map/all_gather | solution.py:181
  9.0 155.7 %all-gather.12.cloned.1.call-start = ((), (), s32[]{:S(2)}) async-start(), calls=%async_computation.9 | async-start | bytes 14155776 | tf_op jit(solution)/shard_map/all_gather | solution.py:211
  93.7 147.4 %all-gather.14.cloned.1.call-start = ((), (), s32[]{:S(2)}) async-start(), calls=%async_computation.10 | async-start | bytes 14155776 | tf_op jit(solution)/shard_map/all_gather | solution.py:212
  96.5 269.4 %all-gather.16.cloned.1.call-start = ((), (), s32[]{:S(2)}) async-start(), calls=%async_computation.11 | async-start | bytes 1216512 | tf_op jit(solution)/shard_map/all_gather | solution.py:182
  97.3 292.0 %all-gather.24.cloned.1.call-start = ((), (), s32[]{:S(2)}) async-start(), calls=%async_computation.15 | async-start | bytes 5308416 | tf_op jit(solution)/shard_map/all_gather | solution.py:188
  98.2 297.7 %all-gather.22.cloned.1.call-start = ((), (), s32[]{:S(2)}) async-start(), calls=%async_computation.14 | async-start | bytes 5308416 | tf_op jit(solution)/shard_map/all_gather | solution.py:186
  98.8 383.7 %all-gather.18.cloned.1.call-start = ((), (), s32[]{:S(2)}) async-start(), calls=%async_computation.12 | async-start | bytes 5308416 | tf_op jit(solution)/shard_map/all_gather | solution.py:187
  100.0 382.6 %all-gather.20.cloned.1.call-start = ((), (), s32[]{:S(2)}) async-start(), calls=%async_computation.13 | async-start | bytes 5308416 | tf_op jit(solution)/shard_map/all_gather | solution.py:189
  384.4 75.9 %all-to-all-start = ((bf16[8,256,768]{2,1,0:T(8,128)(2,1)}), bf16[8,256,768]{2,1,0:T(8,128)(2,1)S(1)}, u32[]{:S(2)}, u32[]{:S(2)}) async-start(bf16[8,256,768]{2,1,0:T(8,128)(2,1)} %select_select_fusion.1), calls=%async_computation | async-start | bytes 6291456 | tf_op jit(solution)/shard_map/all_to_all | solution.py:281
  501.1 74.3 %all-to-all-start.1 = ((bf16[8,256,768]{2,1,0:T(8,128)(2,1)}), bf16[8,256,768]{2,1,0:T(8,128)(2,1)S(1)}, u32[]{:S(2)}, u32[]{:S(2)}) async-start(bf16[8,256,768]{2,1,0:T(8,128)(2,1)} %bitcast.233), calls=%async_computation.1 | async-start | bytes 6291456 | tf_op jit(solution)/shard_map/all_to_all | solution.py:286
  504.9 1293.7 %reduce-scatter.12.cloned.1.call-start = ((), (), s32[]{:S(2)}) async-start(), calls=%async_computation.19 | async-start | bytes 5308416 | tf_op jit(solution)/shard_map/reduce_scatter | solution.py:411
  522.2 296.2 %copy-start.52 = (pred[2048]{0:T(1024)(128)(4,1)}, pred[2048]{0:T(1024)(128)(4,1)S(1)}, u32[]{:S(2)}) copy-start(pred[2048]{0:T(1024)(128)(4,1)S(1)} %get-tuple-element.567) | copy-start | bytes 6148
  735.8 73.1 %all-to-all-start.3 = ((bf16[8,256,768]{2,1,0:T(8,128)(2,1)}), bf16[8,256,768]{2,1,0:T(8,128)(2,1)S(1)}, u32[]{:S(2)}, u32[]{:S(2)}) async-start(bf16[8,256,768]{2,1,0:T(8,128)(2,1)} %bitcast.232), calls=%async_computation.3 | async-start | bytes 6291456 | tf_op jit(solution)/shard_map/all_to_all | solution.py:332
  739.6 1063.5 %reduce-scatter.10.cloned.1.call-start = ((), (), s32[]{:S(2)}) async-start(), calls=%async_computation.18 | async-start | bytes 5308416 | tf_op jit(solution)/shard_map/reduce_scatter | solution.py:408
  748.8 1062.0 %reduce-scatter.8.cloned.1.call-start = ((), (), s32[]{:S(2)}) async-start(), calls=%async_computation.17 | async-start | bytes 2433024 | tf_op jit(solution)/shard_map/reduce_scatter | solution.py:404
  867.3 1001.1 %reduce-scatter.6.cloned.1.call-start = ((), (), s32[]{:S(2)}) async-start(), calls=%async_computation.16 | async-start | bytes 7299072 | tf_op jit(solution)/shard_map/reduce_scatter | solution.py:403
  907.3 25.3 %collective-permute-start.2 = (bf16[4,256,768]{1,2,0:T(8,128)(2,1)}, bf16[4,256,768]{1,2,0:T(8,128)(2,1)}, u32[]{:S(2)}, u32[]{:S(2)}) collective-permute-start(bf16[4,256,768]{1,2,0:T(8,128)(2,1)} %fusion.112), channel_id=1, source_target_pairs={{28,0},{0,4},{4,8},{8,12},{12,16},{16,20},{20,24},{24,28},{29,1},{... | collective-permute-start | bytes 4718600 | tf_op jit(solution)/shard_map/while/body/eval_jaxpr/ppermute | solution.py:29
  910.8 39.7 %collective-permute-start.3 = (bf16[4,256,768]{1,2,0:T(8,128)(2,1)}, bf16[4,256,768]{1,2,0:T(8,128)(2,1)}, u32[]{:S(2)}, u32[]{:S(2)}) collective-permute-start(bf16[4,256,768]{1,2,0:T(8,128)(2,1)} %fusion.113), channel_id=1, source_target_pairs={{28,0},{0,4},{4,8},{8,12},{12,16},{16,20},{20,24},{24,28},{29,1},{... | collective-permute-start | bytes 4718600 | tf_op jit(solution)/shard_map/while/body/eval_jaxpr/ppermute | solution.py:29
  912.3 41.5 %collective-permute-start = (bf16[4,256,768]{1,2,0:T(8,128)(2,1)S(1)}, bf16[4,256,768]{1,2,0:T(8,128)(2,1)S(1)}, u32[]{:S(2)}, u32[]{:S(2)}) collective-permute-start(bf16[4,256,768]{1,2,0:T(8,128)(2,1)S(1)} %copy.230), channel_id=1, source_target_pairs={{0,4},{4,8},{8,12},{12,16},{16,20},{20,24},{24,28},{1,5},{5,9},{9,... | collective-permute-start | bytes 4718600 | tf_op jit(solution)/shard_map/while/body/eval_jaxpr/ppermute | solution.py:23
  914.3 39.5 %collective-permute-start.1 = (bf16[4,256,768]{1,2,0:T(8,128)(2,1)}, bf16[4,256,768]{1,2,0:T(8,128)(2,1)}, u32[]{:S(2)}, u32[]{:S(2)}) collective-permute-start(bf16[4,256,768]{1,2,0:T(8,128)(2,1)} %copy.231), channel_id=1, source_target_pairs={{0,4},{4,8},{8,12},{12,16},{16,20},{20,24},{24,28},{1,5},{5,9},{9,... | collective-permute-start | bytes 4718600 | tf_op jit(solution)/shard_map/while/body/eval_jaxpr/ppermute | solution.py:23
  967.9 71.3 %collective-permute-start.2 = (bf16[4,256,768]{1,2,0:T(8,128)(2,1)}, bf16[4,256,768]{1,2,0:T(8,128)(2,1)}, u32[]{:S(2)}, u32[]{:S(2)}) collective-permute-start(bf16[4,256,768]{1,2,0:T(8,128)(2,1)} %fusion.112), channel_id=1, source_target_pairs={{28,0},{0,4},{4,8},{8,12},{12,16},{16,20},{20,24},{24,28},{29,1},{... | collective-permute-start | bytes 4718600 | tf_op jit(solution)/shard_map/while/body/eval_jaxpr/ppermute | solution.py:29
  1026.4 21.1 %collective-permute-start.3 = (bf16[4,256,768]{1,2,0:T(8,128)(2,1)}, bf16[4,256,768]{1,2,0:T(8,128)(2,1)}, u32[]{:S(2)}, u32[]{:S(2)}) collective-permute-start(bf16[4,256,768]{1,2,0:T(8,128)(2,1)} %fusion.113), channel_id=1, source_target_pairs={{28,0},{0,4},{4,8},{8,12},{12,16},{16,20},{20,24},{24,28},{29,1},{... | collective-permute-start | bytes 4718600 | tf_op jit(solution)/shard_map/while/body/eval_jaxpr/ppermute | solution.py:29
  1028.9 21.9 %collective-permute-start = (bf16[4,256,768]{1,2,0:T(8,128)(2,1)S(1)}, bf16[4,256,768]{1,2,0:T(8,128)(2,1)S(1)}, u32[]{:S(2)}, u32[]{:S(2)}) collective-permute-start(bf16[4,256,768]{1,2,0:T(8,128)(2,1)S(1)} %copy.230), channel_id=1, source_target_pairs={{0,4},{4,8},{8,12},{12,16},{16,20},{20,24},{24,28},{1,5},{5,9},{9,... | collective-permute-start | bytes 4718600 | tf_op jit(solution)/shard_map/while/body/eval_jaxpr/ppermute | solution.py:23
  1030.9 19.9 %collective-permute-start.1 = (bf16[4,256,768]{1,2,0:T(8,128)(2,1)}, bf16[4,256,768]{1,2,0:T(8,128)(2,1)}, u32[]{:S(2)}, u32[]{:S(2)}) collective-permute-start(bf16[4,256,768]{1,2,0:T(8,128)(2,1)} %copy.231), channel_id=1, source_target_pairs={{0,4},{4,8},{8,12},{12,16},{16,20},{20,24},{24,28},{1,5},{5,9},{9,... | collective-permute-start | bytes 4718600 | tf_op jit(solution)/shard_map/while/body/eval_jaxpr/ppermute | solution.py:23
  1064.8 86.5 %collective-permute-start.2 = (bf16[4,256,768]{1,2,0:T(8,128)(2,1)}, bf16[4,256,768]{1,2,0:T(8,128)(2,1)}, u32[]{:S(2)}, u32[]{:S(2)}) collective-permute-start(bf16[4,256,768]{1,2,0:T(8,128)(2,1)} %fusion.112), channel_id=1, source_target_pairs={{28,0},{0,4},{4,8},{8,12},{12,16},{16,20},{20,24},{24,28},{29,1},{... | collective-permute-start | bytes 4718600 | tf_op jit(solution)/shard_map/while/body/eval_jaxpr/ppermute | solution.py:29
  1111.1 43.5 %collective-permute-start.3 = (bf16[4,256,768]{1,2,0:T(8,128)(2,1)}, bf16[4,256,768]{1,2,0:T(8,128)(2,1)}, u32[]{:S(2)}, u32[]{:S(2)}) collective-permute-start(bf16[4,256,768]{1,2,0:T(8,128)(2,1)} %fusion.113), channel_id=1, source_target_pairs={{28,0},{0,4},{4,8},{8,12},{12,16},{16,20},{20,24},{24,28},{29,1},{... | collective-permute-start | bytes 4718600 | tf_op jit(solution)/shard_map/while/body/eval_jaxpr/ppermute | solution.py:29
  1140.1 17.9 collective-permute-start
  1142.1 15.9 collective-permute-start.1
  1172.0 91.5 %collective-permute-start.2 = (bf16[4,256,768]{1,2,0:T(8,128)(2,1)}, bf16[4,256,768]{1,2,0:T(8,128)(2,1)}, u32[]{:S(2)}, u32[]{:S(2)}) collective-permute-start(bf16[4,256,768]{1,2,0:T(8,128)(2,1)} %fusion.112), channel_id=1, source_target_pairs={{28,0},{0,4},{4,8},{8,12},{12,16},{16,20},{20,24},{24,28},{29,1},{... | collective-permute-start | bytes 4718600 | tf_op jit(solution)/shard_map/while/body/eval_jaxpr/ppermute | solution.py:29
  1222.3 44.4 %collective-permute-start.3 = (bf16[4,256,768]{1,2,0:T(8,128)(2,1)}, bf16[4,256,768]{1,2,0:T(8,128)(2,1)}, u32[]{:S(2)}, u32[]{:S(2)}) collective-permute-start(bf16[4,256,768]{1,2,0:T(8,128)(2,1)} %fusion.113), channel_id=1, source_target_pairs={{28,0},{0,4},{4,8},{8,12},{12,16},{16,20},{20,24},{24,28},{29,1},{... | collective-permute-start | bytes 4718600 | tf_op jit(solution)/shard_map/while/body/eval_jaxpr/ppermute | solution.py:29
  1224.8 45.3 %collective-permute-start = (bf16[4,256,768]{1,2,0:T(8,128)(2,1)S(1)}, bf16[4,256,768]{1,2,0:T(8,128)(2,1)S(1)}, u32[]{:S(2)}, u32[]{:S(2)}) collective-permute-start(bf16[4,256,768]{1,2,0:T(8,128)(2,1)S(1)} %copy.230), channel_id=1, source_target_pairs={{0,4},{4,8},{8,12},{12,16},{16,20},{20,24},{24,28},{1,5},{5,9},{9,... | collective-permute-start | bytes 4718600 | tf_op jit(solution)/shard_map/while/body/eval_jaxpr/ppermute | solution.py:23
  1252.2 18.0 collective-permute-start.1
  1284.1 91.5 %collective-permute-start.2 = (bf16[4,256,768]{1,2,0:T(8,128)(2,1)}, bf16[4,256,768]{1,2,0:T(8,128)(2,1)}, u32[]{:S(2)}, u32[]{:S(2)}) collective-permute-start(bf16[4,256,768]{1,2,0:T(8,128)(2,1)} %fusion.112), channel_id=1, source_target_pairs={{28,0},{0,4},{4,8},{8,12},{12,16},{16,20},{20,24},{24,28},{29,1},{... | collective-permute-start | bytes 4718600 | tf_op jit(solution)/shard_map/while/body/eval_jaxpr/ppermute | solution.py:29
  1319.0 59.9 %collective-permute-start.3 = (bf16[4,256,768]{1,2,0:T(8,128)(2,1)}, bf16[4,256,768]{1,2,0:T(8,128)(2,1)}, u32[]{:S(2)}, u32[]{:S(2)}) collective-permute-start(bf16[4,256,768]{1,2,0:T(8,128)(2,1)} %fusion.113), channel_id=1, source_target_pairs={{28,0},{0,4},{4,8},{8,12},{12,16},{16,20},{20,24},{24,28},{29,1},{... | collective-permute-start | bytes 4718600 | tf_op jit(solution)/shard_map/while/body/eval_jaxpr/ppermute | solution.py:29
  1321.5 60.8 %collective-permute-start = (bf16[4,256,768]{1,2,0:T(8,128)(2,1)S(1)}, bf16[4,256,768]{1,2,0:T(8,128)(2,1)S(1)}, u32[]{:S(2)}, u32[]{:S(2)}) collective-permute-start(bf16[4,256,768]{1,2,0:T(8,128)(2,1)S(1)} %copy.230), channel_id=1, source_target_pairs={{0,4},{4,8},{8,12},{12,16},{16,20},{20,24},{24,28},{1,5},{5,9},{9,... | collective-permute-start | bytes 4718600 | tf_op jit(solution)/shard_map/while/body/eval_jaxpr/ppermute | solution.py:23
  1337.8 44.5 %collective-permute-start.1 = (bf16[4,256,768]{1,2,0:T(8,128)(2,1)}, bf16[4,256,768]{1,2,0:T(8,128)(2,1)}, u32[]{:S(2)}, u32[]{:S(2)}) collective-permute-start(bf16[4,256,768]{1,2,0:T(8,128)(2,1)} %copy.231), channel_id=1, source_target_pairs={{0,4},{4,8},{8,12},{12,16},{16,20},{20,24},{24,28},{1,5},{5,9},{9,... | collective-permute-start | bytes 4718600 | tf_op jit(solution)/shard_map/while/body/eval_jaxpr/ppermute | solution.py:23
  1396.2 64.9 %collective-permute-start.2 = (bf16[4,256,768]{1,2,0:T(8,128)(2,1)}, bf16[4,256,768]{1,2,0:T(8,128)(2,1)}, u32[]{:S(2)}, u32[]{:S(2)}) collective-permute-start(bf16[4,256,768]{1,2,0:T(8,128)(2,1)} %fusion.112), channel_id=1, source_target_pairs={{28,0},{0,4},{4,8},{8,12},{12,16},{16,20},{20,24},{24,28},{29,1},{... | collective-permute-start | bytes 4718600 | tf_op jit(solution)/shard_map/while/body/eval_jaxpr/ppermute | solution.py:29
  1419.4 45.1 %collective-permute-start.3 = (bf16[4,256,768]{1,2,0:T(8,128)(2,1)}, bf16[4,256,768]{1,2,0:T(8,128)(2,1)}, u32[]{:S(2)}, u32[]{:S(2)}) collective-permute-start(bf16[4,256,768]{1,2,0:T(8,128)(2,1)} %fusion.113), channel_id=1, source_target_pairs={{28,0},{0,4},{4,8},{8,12},{12,16},{16,20},{20,24},{24,28},{29,1},{... | collective-permute-start | bytes 4718600 | tf_op jit(solution)/shard_map/while/body/eval_jaxpr/ppermute | solution.py:29
  1421.8 46.0 %collective-permute-start = (bf16[4,256,768]{1,2,0:T(8,128)(2,1)S(1)}, bf16[4,256,768]{1,2,0:T(8,128)(2,1)S(1)}, u32[]{:S(2)}, u32[]{:S(2)}) collective-permute-start(bf16[4,256,768]{1,2,0:T(8,128)(2,1)S(1)} %copy.230), channel_id=1, source_target_pairs={{0,4},{4,8},{8,12},{12,16},{16,20},{20,24},{24,28},{1,5},{5,9},{9,... | collective-permute-start | bytes 4718600 | tf_op jit(solution)/shard_map/while/body/eval_jaxpr/ppermute | solution.py:23
  1449.9 18.0 collective-permute-start.1
  1481.8 72.6 %collective-permute-start.2 = (bf16[4,256,768]{1,2,0:T(8,128)(2,1)}, bf16[4,256,768]{1,2,0:T(8,128)(2,1)}, u32[]{:S(2)}, u32[]{:S(2)}) collective-permute-start(bf16[4,256,768]{1,2,0:T(8,128)(2,1)} %fusion.112), channel_id=1, source_target_pairs={{28,0},{0,4},{4,8},{8,12},{12,16},{16,20},{20,24},{24,28},{29,1},{... | collective-permute-start | bytes 4718600 | tf_op jit(solution)/shard_map/while/body/eval_jaxpr/ppermute | solution.py:29
  1516.7 41.0 %collective-permute-start.3 = (bf16[4,256,768]{1,2,0:T(8,128)(2,1)}, bf16[4,256,768]{1,2,0:T(8,128)(2,1)}, u32[]{:S(2)}, u32[]{:S(2)}) collective-permute-start(bf16[4,256,768]{1,2,0:T(8,128)(2,1)} %fusion.113), channel_id=1, source_target_pairs={{28,0},{0,4},{4,8},{8,12},{12,16},{16,20},{20,24},{24,28},{29,1},{... | collective-permute-start | bytes 4718600 | tf_op jit(solution)/shard_map/while/body/eval_jaxpr/ppermute | solution.py:29
  1519.2 41.9 %collective-permute-start = (bf16[4,256,768]{1,2,0:T(8,128)(2,1)S(1)}, bf16[4,256,768]{1,2,0:T(8,128)(2,1)S(1)}, u32[]{:S(2)}, u32[]{:S(2)}) collective-permute-start(bf16[4,256,768]{1,2,0:T(8,128)(2,1)S(1)} %copy.230), channel_id=1, source_target_pairs={{0,4},{4,8},{8,12},{12,16},{16,20},{20,24},{24,28},{1,5},{5,9},{9,... | collective-permute-start | bytes 4718600 | tf_op jit(solution)/shard_map/while/body/eval_jaxpr/ppermute | solution.py:23
  1543.2 18.0 collective-permute-start.1
  1575.1 77.9 %collective-permute-start.2 = (bf16[4,256,768]{1,2,0:T(8,128)(2,1)}, bf16[4,256,768]{1,2,0:T(8,128)(2,1)}, u32[]{:S(2)}, u32[]{:S(2)}) collective-permute-start(bf16[4,256,768]{1,2,0:T(8,128)(2,1)} %fusion.112), channel_id=1, source_target_pairs={{28,0},{0,4},{4,8},{8,12},{12,16},{16,20},{20,24},{24,28},{29,1},{... | collective-permute-start | bytes 4718600 | tf_op jit(solution)/shard_map/while/body/eval_jaxpr/ppermute | solution.py:29
  1610.0 57.3 %collective-permute-start.3 = (bf16[4,256,768]{1,2,0:T(8,128)(2,1)}, bf16[4,256,768]{1,2,0:T(8,128)(2,1)}, u32[]{:S(2)}, u32[]{:S(2)}) collective-permute-start(bf16[4,256,768]{1,2,0:T(8,128)(2,1)} %fusion.113), channel_id=1, source_target_pairs={{28,0},{0,4},{4,8},{8,12},{12,16},{16,20},{20,24},{24,28},{29,1},{... | collective-permute-start | bytes 4718600 | tf_op jit(solution)/shard_map/while/body/eval_jaxpr/ppermute | solution.py:29
  1618.9 51.7 %collective-permute-start = (bf16[4,256,768]{1,2,0:T(8,128)(2,1)S(1)}, bf16[4,256,768]{1,2,0:T(8,128)(2,1)S(1)}, u32[]{:S(2)}, u32[]{:S(2)}) collective-permute-start(bf16[4,256,768]{1,2,0:T(8,128)(2,1)S(1)} %copy.230), channel_id=1, source_target_pairs={{0,4},{4,8},{8,12},{12,16},{16,20},{20,24},{24,28},{1,5},{5,9},{9,... | collective-permute-start | bytes 4718600 | tf_op jit(solution)/shard_map/while/body/eval_jaxpr/ppermute | solution.py:23
  1641.7 29.0 %collective-permute-start.1 = (bf16[4,256,768]{1,2,0:T(8,128)(2,1)}, bf16[4,256,768]{1,2,0:T(8,128)(2,1)}, u32[]{:S(2)}, u32[]{:S(2)}) collective-permute-start(bf16[4,256,768]{1,2,0:T(8,128)(2,1)} %copy.231), channel_id=1, source_target_pairs={{0,4},{4,8},{8,12},{12,16},{16,20},{20,24},{24,28},{1,5},{5,9},{9,... | collective-permute-start | bytes 4718600 | tf_op jit(solution)/shard_map/while/body/eval_jaxpr/ppermute | solution.py:23
  (99 other events, 2215.6 us)
Sparse Core Ops, SparseCore 0:
  11.4 62.8 all-gather.9
  93.9 70.7 all-gather.11
  166.5 74.5 all-gather.13
  244.3 54.0 all-gather.15
  300.8 37.8 all-gather.23
  340.4 38.9 all-gather.21
  381.8 39.7 all-gather.17
  424.0 39.7 all-gather.19
  686.4 51.9 reduce-scatter.11
  748.9 54.1 reduce-scatter.9
  867.4 140.5 reduce-scatter.7
  1687.7 180.7 reduce-scatter.5
where the time goes:
time: 1950 us; the launch traced here: 1940 us
  starting transfers between devices  517 us (27%)
  waiting for transfers between devices  365 us (19%)
  other arithmetic  293 us (15%)
  blocking collectives  283 us (15%)
  matrix products  245 us (13%)
  local copies, waits for them, and re-layouts  208 us (11%)
    ppermute x16, starting transfers between devices, passed_along(): return lax.ppermute(block, axis, route)  310 us
    ppermute x16, starting transfers between devices, from_behind(): return lax.ppermute(block, axis, route)  193 us
    unnamed x1, blocking collectives  100 us
    all_gather x1, waiting for transfers between devices, body(): value_block = lax.all_gather(value_part, 'seq', axis=1, tiled=True)  76.5 us
    all_to_all x1, blocking collectives, body(): lax.all_to_all(grad_dispatch, 'exp', split_axis=0, concat_axis=0, tiled=T...  72.7 us
    all_gather x1, blocking collectives, body(): lax.all_gather(norm_gains.astype(jnp.bfloat16), ('seq', 'exp'), axis=0, t...  69.4 us
    all_to_all x1, waiting for transfers between devices, body(): lax.all_to_all(dispatch, 'exp', split_axis=0, concat_axis=0, tiled=True)  57.8 us
    reduce_scatter x1, waiting for transfers between devices, body(): lax.psum_scatter(input_local, ('seq', 'exp'), scatter_dimension=0, tiled=...  53.9 us
  transfers between devices with their start and end apart: 47, of which 10 were waited for; matrix products, arithmetic and copies ran while one was open for 34% of the time, Pallas kernels for 0%

commit v1 on v0

v1 whole, which is shorter than its diff:
```python
import functools

import jax
import jax.numpy as jnp
from jax import lax
from jax.experimental import pallas as pl
from jax.experimental.pallas import tpu as pltpu
from jax.sharding import PartitionSpec as P

HEAD_DIM = 64
STEP = 10
LANES = 128
BLOCK = 256

norm_eps = 1e-06
beta_one = 0.9
beta_two = 0.999
lamb_eps = 1e-06
decay_rate = 0.01
learn_rate = 0.3
masked_score = -1e30
gelu_scale = 0.7978845608028654
gelu_cubic = 0.044715
flops_per_us = 1.1535e9

f32 = jnp.float32
bf16 = jnp.bfloat16


def struct(shape, dtype):
    return jax.ShapeDtypeStruct(shape, dtype)


def dot(left, right):
    return jnp.dot(left, right, preferred_element_type=f32)


def dot_rows(left, right):
    return lax.dot_general(left, right, (((1,), (1,)), ((), ())), preferred_element_type=f32)


def run_kernel(
    kernel, grid, in_specs, out_specs, out_shape, scratch, span, *operands, after=(), chosen=()
):
    count = len(chosen) + len(in_specs)

    def run(*refs):
        kernel(*refs[:count], *refs[count + len(after) :])

    waited = [pl.BlockSpec(memory_space=pl.ANY) for _ in after]
    return pl.pallas_call(
        run,
        grid_spec=pltpu.PrefetchScalarGridSpec(
            num_scalar_prefetch=len(chosen),
            grid=grid,
            in_specs=list(in_specs) + waited,
            out_specs=out_specs,
            scratch_shapes=scratch,
        ),
        out_shape=out_shape,
        cost_estimate=pl.CostEstimate(
            flops=int(span * flops_per_us), bytes_accessed=0, transcendentals=0
        ),
        compiler_params=pltpu.CompilerParams(
            dimension_semantics=("arbitrary",) * len(grid),
            vmem_limit_bytes=56 * 1024 * 1024,
        ),
    )(*chosen, *operands, *after)


def whole(shape):
    return pl.BlockSpec(shape, lambda *_: (0,) * len(shape))


scalars = pl.BlockSpec(memory_space=pltpu.SMEM)


class Plan:
    def __init__(self, tokens):
        self.n_seq = lax.axis_size("seq")
        self.n_exp = lax.axis_size("exp")
        self.batch, self.pos, self.width = tokens.shape
        self.tokens = self.batch * self.pos
        self.experts = 2 * self.n_exp
        self.cap = 2 * self.tokens // self.experts
        self.rows = self.n_exp * self.cap
        self.pairs = self.width // LANES
        self.per = self.n_seq // self.batch
        self.chunks = -(-self.pairs // self.per)
        self.length = self.n_seq * self.pos

    def rolled(self, chunk):
        turn = self.batch - chunk % self.batch
        return lambda b: lax.rem(b + turn, self.batch)

    def held(self, chunk):
        return [(k, chunk * self.per + k) for k in range(self.per)]

    def used(self, chunk):
        return min(self.per, self.pairs - chunk * self.per)

    def weight_of(self, chunk):
        return 3 * LANES * self.per * chunk


def routing(plan, routes, live):
    tokens, experts, cap, rows = plan.tokens, plan.experts, plan.cap, plan.rows

    def kernel(route_ref, live_ref, slot_ref, count_ref):
        expert = lax.broadcasted_iota(jnp.int32, (experts, tokens), 0)
        alive = live_ref[...] > 0
        hits = [(route_ref[k : k + 1, :] == expert) & alive for k in range(2)]
        hit = jnp.where(hits[0] | hits[1], 1.0, 0.0)
        before = lax.broadcasted_iota(jnp.int32, (tokens, tokens), 0) < lax.broadcasted_iota(
            jnp.int32, (tokens, tokens), 1
        )
        rank = dot(hit.astype(bf16), jnp.where(before, 1.0, 0.0).astype(bf16))
        kept = rank < cap
        base = (expert % 2) * rows + (expert // 2) * cap + 1
        slot = base.astype(f32) + rank
        for k in range(2):
            own = jnp.sum(jnp.where(hits[k] & kept, slot, 0.0), axis=0, keepdims=True)
            slot_ref[k : k + 1, :] = own.astype(jnp.int32) - 1
        total = jnp.sum(jnp.where(kept, hit, 0.0), axis=1, keepdims=True)
        count_ref[...] = jnp.broadcast_to(total, (experts, LANES))

    return run_kernel(
        kernel,
        (1,),
        [whole((2, tokens)), whole((1, tokens))],
        [whole((2, tokens)), whole((experts, LANES))],
        [struct((2, tokens), jnp.int32), struct((experts, LANES), f32)],
        [],
        4,
        routes,
        live,
    )


def project(plan, tokens, gains, weights, after):
    batch, pos, width, chunks = plan.batch, plan.pos, plan.width, plan.chunks

    def kernel(x_ref, gain_ref, w_ref, *out_refs):
        x = x_ref[0].astype(f32)
        factor = lax.rsqrt(jnp.mean(x * x, axis=-1, keepdims=True) + norm_eps)
        normed = (x * factor * gain_ref[0:1, :]).astype(bf16)
        for chunk, out_ref in enumerate(out_refs):
            first, used = plan.weight_of(chunk), plan.used(chunk)
            for part in range(3):
                low = first + part * used * LANES
                made = dot(normed, w_ref[:, low : low + used * LANES])
                if part == 0:
                    made = made.astype(bf16).astype(f32) * HEAD_DIM ** (-0.5)
                made = made.astype(bf16)
                for k in range(plan.per):
                    if k < used:
                        out_ref[k, 0, part] = made[:, k * LANES : (k + 1) * LANES]
                    else:
                        out_ref[k, 0, part] = jnp.zeros((pos, LANES), bf16)

    def chunk_spec(chunk):
        turn = plan.rolled(chunk)
        return pl.BlockSpec((plan.per, 1, 3, pos, LANES), lambda b: (0, turn(b), 0, 0, 0))

    return list(
        run_kernel(
            kernel,
            (batch,),
            [
                pl.BlockSpec((1, pos, width), lambda b: (b, 0, 0)),
                whole((2, width)),
                whole(weights.shape),
            ],
            [chunk_spec(c) for c in range(chunks)],
            [struct((plan.per, batch, 3, pos, LANES), bf16)] * chunks,
            [],
            8,
            tokens,
            gains,
            weights,
            after=after,
        )
    )


def over_seq(values):
    return lax.all_to_all(values, "seq", split_axis=0, concat_axis=0, tiled=True)


def sent(blocks):
    return [shifted(block, k) if k else block for k, block in enumerate(blocks)]


def sent_back(blocks):
    return [shifted(block, len(blocks) - k) if k else block for k, block in enumerate(blocks)]


def shifted(values, distance):
    count = lax.axis_size("exp")
    return lax.ppermute(values, "exp", [(i, (i + distance) % count) for i in range(count)])


def lane_masks():
    lane = lax.broadcasted_iota(jnp.int32, (1, LANES), 1)
    first = jnp.where(lane < HEAD_DIM, 1.0, 0.0)
    return first.astype(bf16), (1.0 - first).astype(bf16)


def allowed_block(key_block, query_block, length):
    key_pos = key_block * BLOCK + lax.broadcasted_iota(jnp.int32, (BLOCK, BLOCK), 0)
    query_pos = query_block * BLOCK + lax.broadcasted_iota(jnp.int32, (BLOCK, BLOCK), 1)
    return (key_pos <= query_pos) & (key_pos < length)


def attend(plan, packed, length, after):
    pos, n_seq = plan.pos, plan.n_seq
    blocks, group = plan.length // BLOCK, BLOCK // pos

    def kernel(length_ref, x_ref, out_ref, log_ref, values_t):
        query_block = pl.program_id(0)
        length = length_ref[0]

        def read(block, part):
            return x_ref[pl.ds(block * group, group), part].reshape(BLOCK, LANES)

        @pl.when(query_block == 0)
        def _():
            for block in range(blocks):
                values_t[block] = read(block, 2).astype(f32).T.astype(bf16)

        query = read(query_block, 0)
        queries = [query * mask for mask in lane_masks()]

        def fold(key_blocks, state, allowed=None):
            scores = [
                [dot_rows(read(block, 1), query) for block in key_blocks] for query in queries
            ]
            after = []
            for head in range(2):
                parts = scores[head]
                if allowed is not None:
                    parts = [jnp.where(allowed, score, masked_score) for score in parts]
                peak = functools.reduce(jnp.maximum, parts)
                peak = jnp.max(peak, axis=0, keepdims=True)
                if state is not None:
                    peak = jnp.maximum(state[head][0], peak)
                weights = [jnp.exp(score - peak) for score in parts]
                total = jnp.sum(sum(weights), axis=0, keepdims=True)
                added = sum(
                    dot(
                        values_t[block, head * HEAD_DIM : (head + 1) * HEAD_DIM, :],
                        weight.astype(bf16),
                    )
                    for block, weight in zip(key_blocks, weights)
                )
                if state is not None:
                    old_peak, old_total, old_sum = state[head]
                    shrink = jnp.exp(old_peak - peak)
                    total = old_total * shrink + total
                    added = old_sum * shrink + added
                after.append((peak, total, added))
            return tuple(after)

        inner = lax.min(query_block, length // BLOCK)
        state = fold([inner], None, allowed_block(inner, query_block, length))
        odd = lax.rem(inner, 2)
        state = lax.fori_loop(0, odd, lambda i, state: fold([i], state), state)
        state = lax.fori_loop(
            0, inner // 2, lambda i, state: fold([odd + 2 * i, odd + 2 * i + 1], state), state
        )
        context = jnp.concatenate([added / total for _, total, added in state], axis=0)
        out_ref[...] = context.T.astype(bf16).reshape(group, pos, LANES)
        for head in range(2):
            peak, total, _ = state[head]
            log_ref[0, head : head + 1, :] = peak + jnp.log(total)

    return run_kernel(
        kernel,
        (blocks,),
        [scalars, whole((n_seq, 3, pos, LANES))],
        [
            pl.BlockSpec((group, pos, LANES), lambda i: (i, 0, 0)),
            pl.BlockSpec((1, 2, BLOCK), lambda i: (i, 0, 0)),
        ],
        [struct((n_seq, pos, LANES), bf16), struct((blocks, 2, BLOCK), f32)],
        [pltpu.VMEM((blocks, LANES, BLOCK), bf16)],
        20,
        length,
        packed,
        after=after,
    )


def attend_back(plan, packed, context, context_grad, log_total, length, after):
    pos, n_seq = plan.pos, plan.n_seq
    blocks, group = plan.length // BLOCK, BLOCK // pos

    def kernel(
        length_ref, x_ref, c_ref, g_ref, log_ref, out_ref, keys_t, queries, grads, delta, query_grad
    ):
        key_block = pl.program_id(0)
        length = length_ref[0]

        def read(ref, block, *part):
            return ref[(pl.ds(block * group, group), *part)].reshape(BLOCK, LANES)

        @pl.when(key_block == 0)
        def _():
            masks = lane_masks()
            for block in range(blocks):
                keys_t[block] = read(x_ref, block, 1).astype(f32).T.astype(bf16)
                query, grad = read(x_ref, block, 0), read(g_ref, block)
                for head in range(2):
                    queries[head, block] = query * masks[head]
                    grads[head, block] = grad * masks[head]
                product = (read(c_ref, block).astype(f32) * grad.astype(f32)).T
                for head in range(2):
                    delta[block, head : head + 1, :] = jnp.sum(
                        product[head * HEAD_DIM : (head + 1) * HEAD_DIM], axis=0, keepdims=True
                    )
                query_grad[block] = jnp.zeros((LANES, BLOCK), f32)

        key = read(x_ref, key_block, 1)
        value = read(x_ref, key_block, 2)
        key_t = keys_t[key_block]

        def fold(masked, query_blocks, state):
            key_grad, value_grad = state
            chains = [(block, head) for block in query_blocks for head in range(2)]
            scores = [dot_rows(key, queries[head, block]) for block, head in chains]
            products = [dot_rows(value, grads[head, block]) for block, head in chains]
            made = []
            for (block, head), score, product in zip(chains, scores, products):
                weight = jnp.exp(score - log_ref[block, head : head + 1, :])
                if masked:
                    weight = jnp.where(allowed_block(key_block, block, length), weight, 0.0)
                value_grad = value_grad + dot(weight.astype(bf16), grads[head, block])
                score_grad = weight * (product - delta[block, head : head + 1, :])
                score_grad = score_grad.astype(bf16)
                key_grad = key_grad + dot(score_grad, queries[head, block])
                made.append(dot(key_t[head * HEAD_DIM : (head + 1) * HEAD_DIM], score_grad))
            for (block, head), part in zip(chains, made):
                query_grad[block, pl.ds(head * HEAD_DIM, HEAD_DIM), :] += part
            return key_grad, value_grad

        zero = jnp.zeros((BLOCK, LANES), f32)

        def store(state):
            for part in range(2):
                out_ref[pl.ds(key_block * group, group), 1 + part] = (
                    state[part].astype(bf16).reshape(group, pos, LANES)
                )

        first = key_block * BLOCK
        inside = first + BLOCK <= length

        @pl.when(inside)
        def _():
            state = fold(True, [key_block], (zero, zero))
            odd = lax.rem(blocks - 1 - key_block, 2)
            state = lax.fori_loop(
                0, odd, lambda i, state: fold(False, [key_block + 1 + i], state), state
            )
            start = key_block + 1 + odd
            pairs = (blocks - start) // 2
            store(
                lax.fori_loop(
                    0,
                    pairs,
                    lambda i, state: fold(False, [start + 2 * i, start + 2 * i + 1], state),
                    state,
                )
            )

        @pl.when(jnp.logical_not(inside) & (first < length))
        def _():
            store(
                lax.fori_loop(
                    key_block, blocks, lambda i, state: fold(True, [i], state), (zero, zero)
                )
            )

        @pl.when(first >= length)
        def _():
            store((zero, zero))

        @pl.when(key_block == blocks - 1)
        def _():
            for block in range(blocks):
                grad = query_grad[block].T * HEAD_DIM ** (-0.5)
                out_ref[block * group : (block + 1) * group, 0] = grad.astype(bf16).reshape(
                    group, pos, LANES
                )

    return run_kernel(
        kernel,
        (blocks,),
        [
            scalars,
            whole((n_seq, 3, pos, LANES)),
            whole((n_seq, pos, LANES)),
            pl.BlockSpec((n_seq, None, pos, LANES), lambda i: (0, context_grad[1], 0, 0)),
            whole((blocks, 2, BLOCK)),
        ],
        whole((n_seq, 3, pos, LANES)),
        struct((n_seq, 3, pos, LANES), bf16),
        [
            pltpu.VMEM((blocks, LANES, BLOCK), bf16),
            pltpu.VMEM((2, blocks, BLOCK, LANES), bf16),
            pltpu.VMEM((2, blocks, BLOCK, LANES), bf16),
            pltpu.VMEM((blocks, 2, BLOCK), f32),
            pltpu.VMEM((blocks, LANES, BLOCK), f32),
        ],
        22,
        length,
        packed,
        context,
        context_grad[0],
        log_total,
        after=after,
    )


def chunk_block(plan, chunk):
    turn = plan.rolled(chunk)
    return pl.BlockSpec((plan.per, 1, plan.pos, LANES), lambda b: (0, turn(b), 0, 0))


def joined_block(plan, chunk, index):
    turn = plan.rolled(chunk)
    block = (plan.per, 1, 1, plan.pos, LANES)
    return pl.BlockSpec(block, lambda b: (0, turn(b), index, 0, 0))


def token_block(plan):
    return pl.BlockSpec((1, plan.pos, plan.width), lambda b: (b, 0, 0))


def combine_heads(plan, tokens, contexts, gains, weights):
    batch, pos, width, chunks = plan.batch, plan.pos, plan.width, plan.chunks

    def kernel(x_ref, gain_ref, w_ref, *refs):
        context_refs, outs = refs[:chunks], refs[chunks:]
        context_ref, middle_ref, normed_ref, scaled_ref = outs
        parts = [
            context_refs[chunk][k, 0, 0]
            for chunk in range(chunks)
            for k, pair in plan.held(chunk)
            if pair < plan.pairs
        ]
        context = jnp.concatenate(parts, axis=1)
        context_ref[0] = context
        x = x_ref[0].astype(f32)
        factor = lax.rsqrt(jnp.mean(x * x, axis=-1, keepdims=True) + norm_eps)
        scaled_ref[0] = (x * factor).astype(bf16)
        middle = x + dot(context, w_ref[...])
        middle_ref[0] = middle
        factor = lax.rsqrt(jnp.mean(middle * middle, axis=-1, keepdims=True) + norm_eps)
        normed_ref[0] = (middle * factor * gain_ref[1:2, :]).astype(bf16)

    return run_kernel(
        kernel,
        (batch,),
        [
            token_block(plan),
            whole((2, width)),
            whole((width, width)),
        ]
        + [joined_block(plan, c, index) for c, (_, index) in enumerate(contexts)],
        [token_block(plan)] * 4,
        [struct((batch, pos, width), kind) for kind in (bf16, f32, bf16, bf16)],
        [],
        6,
        tokens,
        gains,
        weights,
        *[values for values, _ in contexts],
    )


def dispatch(plan, which, rows, slots, place):
    cap, tokens, width, n_exp = plan.cap, plan.tokens, plan.width, plan.n_exp

    def kernel(place_ref, slot_ref, row_ref, *out_refs):
        for k, out_ref in enumerate(out_refs):
            first = which * plan.rows + lax.rem(place_ref[0] + k, n_exp) * cap
            slot = first + lax.broadcasted_iota(jnp.int32, (cap, tokens), 0)
            taken = (slot_ref[0:1, :] == slot) | (slot_ref[1:2, :] == slot)
            choice = jnp.where(taken, 1.0, 0.0).astype(bf16)
            out_ref[...] = dot(choice, row_ref[...]).astype(bf16)

    return run_kernel(
        kernel,
        (1,),
        [scalars, whole((2, tokens)), whole((tokens, width))],
        [whole((cap, width))] * n_exp,
        [struct((cap, width), bf16)] * n_exp,
        [],
        5,
        place,
        slots,
        rows,
    )


def dispatch_grads(plan, rows, slots, gates, place):
    cap, tokens, width, n_exp = plan.cap, plan.tokens, plan.width, plan.n_exp

    def kernel(place_ref, slot_ref, gate_ref, row_ref, *out_refs):
        for index, out_ref in enumerate(out_refs):
            group = lax.rem(place_ref[0] + index % n_exp, n_exp)
            first = (index // n_exp) * plan.rows + group * cap
            slot = first + lax.broadcasted_iota(jnp.int32, (cap, tokens), 0)
            taken = [slot_ref[k : k + 1, :] == slot for k in range(2)]
            gate = jnp.where(
                taken[0], gate_ref[0:1, :], jnp.where(taken[1], gate_ref[1:2, :], 0.0)
            )
            gate = jnp.sum(gate, axis=1, keepdims=True)
            choice = jnp.where(taken[0] | taken[1], 1.0, 0.0).astype(bf16)
            out_ref[...] = (dot(choice, row_ref[...]) * gate).astype(bf16)

    made = run_kernel(
        kernel,
        (1,),
        [scalars, whole((2, tokens)), whole((2, tokens)), whole((tokens, width))],
        [whole((cap, width))] * (2 * n_exp),
        [struct((cap, width), bf16)] * (2 * n_exp),
        [],
        8,
        place,
        slots,
        gates,
        rows,
    )
    return made[:n_exp], made[n_exp:]


def pack_expert(matrix_in, matrix_out):
    rows, width = matrix_in.shape[0], matrix_out.shape[1]
    steps = matrix_in.shape[1] // width

    def kernel(in_ref, out_ref, packed_ref):
        for step in range(steps):
            packed_ref[step] = in_ref[:, step * width : (step + 1) * width].astype(bf16)
            packed_ref[steps + step] = out_ref[step * rows : (step + 1) * rows, :].astype(bf16)

    return run_kernel(
        kernel,
        (1,),
        [whole(matrix_in.shape), whole(matrix_out.shape)],
        whole((2 * steps, rows, width)),
        struct((2 * steps, rows, width), bf16),
        [],
        2,
        matrix_in,
        matrix_out,
    )


class ExpertLayout:
    def __init__(self, plan, blocks):
        self.n_seq, count, self.rows, self.width = blocks.shape
        self.steps = count // 2
        self.share = self.n_seq // self.steps
        self.direct = self.rows % 16 == 0
        if self.direct:
            self.operands = [blocks, blocks]
            self.in_spec = pl.BlockSpec(
                (self.n_seq, 1, self.rows, self.width), lambda f: (0, f, 0, 0)
            )
            self.out_spec = pl.BlockSpec(
                (self.share, self.steps, self.rows, self.width), lambda f: (f, 1, 0, 0)
            )
            self.in_tile = (self.n_seq, 1, self.rows, self.width)
            self.out_tile = (self.share, self.steps, self.rows, self.width)
        else:
            tile = (1, 1, self.width, self.width)
            first = blocks[:, : self.steps].transpose(1, 0, 2, 3)
            second = blocks[:, self.steps :]
            shape = (1, self.steps, self.width, self.width)
            self.operands = [first.reshape(shape), second.reshape(shape)]
            self.in_spec = pl.BlockSpec(tile, lambda f: (0, f, 0, 0))
            self.out_spec = self.in_spec


def run_expert(plan, trainable, rows, grads, layout, after):
    cap, width, steps, groups = plan.cap, plan.width, layout.steps, len(rows)
    count = groups * cap

    def kernel(*refs):
        refs = list(refs)

        def next_refs(number):
            return [refs.pop(0) for _ in range(number)]

        x_refs, g_refs, (in_ref, out_ref) = next_refs(groups), next_refs(groups), next_refs(2)
        copy_refs, result_refs = next_refs(groups), next_refs(groups)
        active, active_grad, copy_sum, result_sum = refs
        step = pl.program_id(0)

        @pl.when(step == 0)
        def _():
            copy_sum[...] = jnp.zeros_like(copy_sum)
            result_sum[...] = jnp.zeros_like(result_sum)

        weight_in = in_ref[...].reshape(width, width)
        weight_out = out_ref[...].reshape(width, width)
        for k in range(groups):
            part = slice(k * cap, (k + 1) * cap)
            hidden = dot(x_refs[k][...], weight_in)
            back = dot_rows(g_refs[k][...], weight_out)
            square = hidden * hidden
            bend = jnp.tanh(gelu_scale * hidden * (1.0 + gelu_cubic * square))
            half = 0.5 * (1.0 + bend)
            slope = half + 0.5 * hidden * (1.0 - bend * bend) * (
                gelu_scale + 3.0 * gelu_scale * gelu_cubic * square
            )
            active[part] = (hidden * half).astype(bf16)
            active_grad[part] = (back * slope).astype(bf16)
            copy_sum[part] += dot_rows(active_grad[part], weight_in)
            result_sum[part] += dot(active[part], weight_out)

        @pl.when(step == steps - 1)
        def _():
            for k in range(groups):
                part = slice(k * cap, (k + 1) * cap)
                copy_refs[k][...] = copy_sum[part].astype(bf16)
                result_refs[k][...] = result_sum[part].astype(bf16)

    row_blocks = [whole((cap, width))] * groups
    row_structs = [struct((cap, width), bf16)] * groups
    sums = [pltpu.VMEM((count, width), f32)] * 2
    hidden_specs, hidden_shapes, hidden_scratch = [], [], [pltpu.VMEM((count, width), bf16)] * 2
    if trainable:
        hidden_specs = [pl.BlockSpec((count, width), lambda f: (0, f))] * 2
        hidden_shapes = [struct((count, steps * width), bf16)] * 2
        hidden_scratch = []
    made = run_kernel(
        kernel,
        (steps,),
        row_blocks * 2 + [layout.in_spec, layout.out_spec],
        row_blocks * 2 + hidden_specs,
        row_structs * 2 + hidden_shapes,
        hidden_scratch + sums,
        7 * groups,
        *rows,
        *grads,
        *layout.operands,
        after=after,
    )
    made = list(made)
    return made[:groups], made[groups : 2 * groups], made[2 * groups :]


def expert_weight_grads(plan, rows, grads, hidden, layout, after):
    cap, width, n_exp, count, steps = plan.cap, plan.width, plan.n_exp, plan.rows, layout.steps
    shape = (layout.n_seq, 2 * steps, layout.rows, width)
    parts = len(hidden) // 2

    def kernel(*refs):
        x_refs, g_refs = refs[:n_exp], refs[n_exp : 2 * n_exp]
        hidden_refs, refs = refs[2 * n_exp : 2 * n_exp + 2 * parts], refs[2 * n_exp + 2 * parts :]
        out_ref, rows_t, grads_t = refs
        step = pl.program_id(0)

        @pl.when(step == 0)
        def _():
            for k in range(n_exp):
                rows_t[:, k * cap : (k + 1) * cap] = x_refs[k][...].T
                grads_t[:, k * cap : (k + 1) * cap] = g_refs[k][...].T

        inner, outer, first = 0.0, 0.0, 0
        for part in range(parts):
            active, active_grad = hidden_refs[2 * part : 2 * part + 2]
            span = slice(first, first + active.shape[0])
            inner = inner + dot(rows_t[:, span], active_grad[...])
            outer = outer + dot(grads_t[:, span], active[...])
            first = first + active.shape[0]
        inner, outer = inner.astype(bf16), outer.T.astype(bf16)
        if layout.direct:
            out_ref[:, pl.ds(step, 1)] = inner.reshape(layout.in_tile)
            out_ref[pl.ds(step * layout.share, layout.share), steps:] = outer.reshape(
                layout.out_tile
            )
        else:
            out_ref[0, step] = inner
            out_ref[1, step] = outer

    out_shape = shape if layout.direct else (2, steps, width, width)
    made = run_kernel(
        kernel,
        (steps,),
        [whole((cap, width))] * (2 * n_exp)
        + [pl.BlockSpec((values.shape[0], width), lambda f: (0, f)) for values in hidden],
        whole(out_shape),
        struct(out_shape, bf16),
        [pltpu.VMEM((width, count), bf16)] * 2,
        16,
        *rows,
        *grads,
        *hidden,
        after=after,
    )
    if layout.direct:
        return made
    inner = made[0].reshape(steps, layout.n_seq, layout.rows, width).transpose(1, 0, 2, 3)
    outer = made[1].reshape(layout.n_seq, steps, layout.rows, width)
    return jnp.concatenate([inner, outer], axis=1)


def held_until(values, waited):
    anywhere = pl.BlockSpec(memory_space=pl.ANY)
    held = pl.pallas_call(
        lambda *refs: None,
        in_specs=[anywhere] * (len(values) + len(waited)),
        out_specs=[anywhere] * len(values),
        out_shape=[struct(value.shape, value.dtype) for value in values],
        input_output_aliases={index: index for index in range(len(values))},
        cost_estimate=pl.CostEstimate(flops=0, bytes_accessed=0, transcendentals=0),
    )(*values, *waited)
    return list(held)


def norm_back(values, gain, grad):
    factor = lax.rsqrt(jnp.mean(values * values, axis=-1, keepdims=True) + norm_eps)
    scaled = values * factor
    inner = grad * gain
    slide = jnp.mean(inner * scaled, axis=-1, keepdims=True)
    return (inner - scaled * slide) * factor, jnp.sum(grad * scaled, axis=0, keepdims=True)


def chosen(slot_ref, slots, k):
    index = lax.broadcasted_iota(jnp.int32, (slot_ref.shape[0], slots), 1)
    return slot_ref[:, k : k + 1] == index


def join_rows(refs, joined):
    rows = refs[0].shape[0]
    for index, ref in enumerate(refs):
        joined[index * rows : (index + 1) * rows] = ref[...]


def turn_back(plan, returned, slots, middle, cotangent, context, gains, weights, after):
    batch, pos, width, chunks, cap = plan.batch, plan.pos, plan.width, plan.chunks, plan.cap
    groups = 2 * plan.n_exp

    def kernel(slot_ref, m_ref, y_ref, c_ref, gain_ref, w_ref, *refs):
        back_refs, refs = refs[:groups], refs[groups:]
        grad_ref, output_ref, gain_grad_ref = refs[:3]
        context_grad_refs, (joined, output_sum, gain_sum) = refs[3 : 3 + chunks], refs[3 + chunks :]
        b = pl.program_id(0)

        @pl.when(b == 0)
        def _():
            output_sum[...] = jnp.zeros_like(output_sum)
            gain_sum[...] = jnp.zeros_like(gain_sum)
            join_rows(back_refs, joined)

        choice = chosen(slot_ref, groups * cap, 0) | chosen(slot_ref, groups * cap, 1)
        second_grad = dot(jnp.where(choice, 1.0, 0.0).astype(bf16), joined[...])
        part, gain_grad = norm_back(m_ref[0], gain_ref[1:2, :], second_grad)
        middle_grad = y_ref[0].astype(f32) + part
        grad_ref[0] = middle_grad
        gain_sum[...] += gain_grad
        branch = middle_grad.astype(bf16)
        context_grad = dot_rows(branch, w_ref[...]).astype(bf16)
        for chunk in range(chunks):
            for k, pair in plan.held(chunk):
                if pair < plan.pairs:
                    made = context_grad[:, pair * LANES : (pair + 1) * LANES]
                else:
                    made = jnp.zeros((pos, LANES), bf16)
                context_grad_refs[chunk][k, 0] = made
        output_sum[...] += dot(c_ref[0].T, branch)

        @pl.when(b == batch - 1)
        def _():
            output_ref[:, :width] = output_sum[...].astype(bf16)
            column = jnp.broadcast_to(gain_sum[...], (LANES, width)).T
            output_ref[:, width:] = column.astype(bf16)
            gain_grad_ref[...] = gain_sum[...]

    return run_kernel(
        kernel,
        (batch,),
        [
            pl.BlockSpec((pos, 2), lambda b: (b, 0)),
            token_block(plan),
            token_block(plan),
            token_block(plan),
            whole((2, width)),
            whole((width, width)),
        ]
        + [whole((cap, width))] * groups,
        [token_block(plan), whole((width, width + LANES)), whole((1, width))]
        + [chunk_block(plan, c) for c in range(chunks)],
        [
            struct((batch, pos, width), f32),
            struct((width, width + LANES), bf16),
            struct((1, width), f32),
        ]
        + [struct((plan.per, batch, pos, LANES), bf16)] * chunks,
        [
            pltpu.VMEM((groups * cap, width), bf16),
            pltpu.VMEM((width, width), f32),
            pltpu.VMEM((1, width), f32),
        ],
        12,
        slots,
        middle,
        cotangent,
        context,
        gains,
        weights,
        *returned,
        after=after,
    )


def mix_results(plan, returned, slots, gates, middle, after):
    batch, pos, width, cap = plan.batch, plan.pos, plan.width, plan.cap
    groups = 2 * plan.n_exp

    def kernel(slot_ref, gate_ref, m_ref, *refs):
        back_refs, out_ref, joined = refs[:groups], refs[groups], refs[groups + 1]

        @pl.when(pl.program_id(0) == 0)
        def _():
            join_rows(back_refs, joined)

        total = m_ref[0]
        for k in range(2):
            choice = jnp.where(chosen(slot_ref, groups * cap, k), 1.0, 0.0).astype(bf16)
            total = total + dot(choice, joined[...]) * gate_ref[:, k : k + 1]
        out_ref[0] = total.astype(bf16)

    return run_kernel(
        kernel,
        (batch,),
        [
            pl.BlockSpec((pos, 2), lambda b: (b, 0)),
            pl.BlockSpec((pos, 2), lambda b: (b, 0)),
            token_block(plan),
        ]
        + [whole((cap, width))] * groups,
        token_block(plan),
        struct((batch, pos, width), bf16),
        [pltpu.VMEM((groups * cap, width), bf16)],
        10,
        slots,
        gates,
        middle,
        *returned,
        after=after,
    )


def unit_weight_grads(plan, packed_grads, normed, weights, units, after):
    pos, width, n_seq, chunks = plan.pos, plan.width, plan.n_seq, plan.chunks
    wide = 3 * LANES
    steps = 2
    share = n_seq // steps

    def kernel(unit_ref, *refs):
        g_refs, n_ref, refs = refs[:chunks], refs[chunks], refs[chunks + 1 :]
        w_refs, (out_ref, total, gain_sum) = refs[: 3 * chunks], refs[3 * chunks :]
        step = pl.program_id(1)

        def chunk_step(chunk):
            made = jnp.concatenate(
                [g_refs[chunk][:, part].reshape(share * pos, LANES).T for part in range(3)],
                axis=0,
            )
            made = dot(made, n_ref[:, 0].reshape(share * pos, width))

            @pl.when(step == 0)
            def _():
                total[...] = made

            @pl.when(step == steps - 1)
            def _():
                done = (total[...] + made).T
                out_ref[:, chunk * wide : (chunk + 1) * wide] = done.astype(bf16)
                held = [ref[...].astype(f32) for ref in w_refs[3 * chunk : 3 * chunk + 3]]
                gain = jnp.sum(done * jnp.concatenate(held, axis=1), axis=1, keepdims=True)
                gain = jnp.broadcast_to(gain, (width, LANES))
                if chunk:
                    gain = gain_sum[...] + gain
                gain_sum[...] = gain
                if chunk == chunks - 1:
                    out_ref[:, chunks * wide :] = gain.astype(bf16)

        for chunk in range(chunks):
            pl.when(pl.program_id(0) == chunk)(functools.partial(chunk_step, chunk))

    def grad_block(chunk):
        def place(c, s, unit):
            s = jnp.where(c == chunk, s, jnp.where(c < chunk, 0, steps - 1))
            return (s, 0, 0, 0)

        return pl.BlockSpec((share, 3, pos, LANES), place)

    def weight_block(chunk, part):
        first, used = plan.weight_of(chunk) // LANES, plan.used(chunk)

        def place(c, s, unit):
            return (0, first + part * used + lax.min(unit[chunks], used - 1))

        return pl.BlockSpec((width, LANES), place)

    held = [(chunk, part) for chunk in range(chunks) for part in range(3)]
    out_wide = chunks * wide + LANES
    return run_kernel(
        kernel,
        (chunks, steps),
        [grad_block(chunk) for chunk in range(chunks)]
        + [pl.BlockSpec((share, 1, pos, width), lambda c, s, unit: (s, unit[c], 0, 0))]
        + [weight_block(chunk, part) for chunk, part in held],
        whole((width, out_wide)),
        struct((width, out_wide), bf16),
        [pltpu.VMEM((wide, width), f32), pltpu.VMEM((width, LANES), f32)],
        13,
        *packed_grads,
        normed,
        *[weights] * len(held),
        chosen=[units],
        after=after,
    )


def project_back(plan, packed_grads, tokens, gains, weights, middle_grad):
    batch, pos, width, chunks = plan.batch, plan.pos, plan.width, plan.chunks

    def kernel(x_ref, gain_ref, m_ref, w_ref, *refs):
        g_refs, out_ref = refs[:chunks], refs[chunks]
        first_grad = 0.0
        for chunk in range(chunks):
            used = plan.used(chunk)
            made = jnp.concatenate(
                [g_refs[chunk][k, 0, part] for part in range(3) for k in range(used)], axis=1
            )
            first = plan.weight_of(chunk)
            weight = w_ref[:, first : first + 3 * used * LANES]
            first_grad = first_grad + dot_rows(made, weight)
        piece, _ = norm_back(x_ref[0].astype(f32), gain_ref[0:1, :], first_grad)
        out_ref[0] = m_ref[0] + piece

    def chunk_spec(chunk):
        turn = plan.rolled(chunk)
        return pl.BlockSpec((plan.per, 1, 3, pos, LANES), lambda b: (0, turn(b), 0, 0, 0))

    return run_kernel(
        kernel,
        (batch,),
        [token_block(plan), whole((2, width)), token_block(plan), whole(weights.shape)]
        + [chunk_spec(c) for c in range(chunks)],
        token_block(plan),
        struct((batch, pos, width), f32),
        [],
        10,
        tokens,
        gains,
        middle_grad,
        weights,
        *packed_grads,
    )


def lamb_update(weight, grad, first, second, decay):
    first_new = beta_one * first + (1.0 - beta_one) * grad
    second_new = beta_two * second + (1.0 - beta_two) * grad * grad
    update = (
        first_new
        / (1.0 - beta_one**STEP)
        / (jnp.sqrt(second_new / (1.0 - beta_two**STEP)) + lamb_eps)
        + decay * weight
    )
    return (first_new, second_new, update)


def square_pair(weight, update):
    return jnp.stack([jnp.sum(weight * weight), jnp.sum(update * update)])


def fold_rows(plan, received, output_sums, place, after):
    batch, per, n_exp = plan.batch, plan.per, plan.n_exp
    rows, wide = received.shape[2:]
    other = output_sums.shape[2]

    def kernel(place_ref, r_ref, o_ref, *out_refs):
        for k, out_ref in enumerate(out_refs):
            group = lax.rem(place_ref[0] + k, n_exp)
            for p in range(per):
                total = 0.0
                for b in range(batch):
                    total = total + r_ref[p * batch + b, group].astype(f32)
                out_ref[:, p * wide : (p + 1) * wide] = total.astype(bf16)
            out_ref[:, per * wide :] = o_ref[group]

    return run_kernel(
        kernel,
        (1,),
        [scalars, whole(received.shape), whole(output_sums.shape)],
        [whole((rows, per * wide + other))] * n_exp,
        [struct((rows, per * wide + other), bf16)] * n_exp,
        [],
        3,
        place,
        received,
        output_sums,
        after=after,
    )


def lamb_rows(plan, blocks, weights, known, after):
    n_exp, width, per, chunks = plan.n_exp, plan.width, plan.per, plan.chunks
    rows = blocks[0].shape[0]
    wide = 3 * LANES * chunks + LANES
    devices = plan.n_seq * n_exp
    decays = (decay_rate, decay_rate, 0.0)

    def kernel(*refs):
        block_refs, refs = refs[:n_exp], refs[n_exp:]
        weight_refs, known_ref, refs = refs[:9], refs[9], refs[10:]
        out_refs, sums_ref = refs[:12], refs[12]

        def total(low, high):
            return sum(ref[:, low:high].astype(f32) for ref in block_refs)

        def place_of(part, pair):
            chunk, p = pair // per, pair % per
            return p * wide + (chunk * 3 + part) * LANES

        input_grad = jnp.concatenate(
            [
                total(place_of(part, pair), place_of(part, pair) + LANES)
                for part in range(3)
                for pair in range(plan.pairs)
            ],
            axis=1,
        )
        input_grad = input_grad * weight_refs[6][:, 0:1].astype(bf16).astype(f32)
        first = per * wide
        output_grad = total(first, first + width)
        expert_gain = total(first + width, first + width + LANES)
        attend_gain = sum(total(p * wide + wide - LANES, (p + 1) * wide) for p in range(per))
        gains_grad = jnp.concatenate([attend_gain[:, 0:1], expert_gain[:, 0:1]], axis=1)

        lane = lax.broadcasted_iota(jnp.int32, (1, LANES), 1)
        sums = known_ref[...]
        for index, grad in enumerate((input_grad, output_grad, gains_grad)):
            weight, moment, square = [ref[...] for ref in weight_refs[3 * index : 3 * index + 3]]
            moment, square, update = lamb_update(weight, grad, moment, square, decays[index])
            for ref, value in zip(out_refs[4 * index :], (grad, moment, square, update)):
                ref[...] = value
            for side, value in enumerate((weight, update)):
                parts = [value] if index < 2 else [value[:, 0:1], value[:, 1:2]]
                for part, column in enumerate(parts):
                    found = jnp.sum(column * column, axis=(0, 1), keepdims=True)
                    sums = sums + jnp.where(lane == 2 * (index + part) + side, found, 0.0)
        sums_ref[...] = jnp.broadcast_to(sums[None], sums_ref.shape)

    shapes = [weight.shape for weight in weights]
    outs = [shape for shape in shapes[::3] for _ in range(4)]
    return run_kernel(
        kernel,
        (1,),
        [whole(blocks[0].shape)] * n_exp + [whole(shape) for shape in shapes] + [whole((1, LANES))],
        [whole(shape) for shape in outs] + [whole((devices, 8, LANES))],
        [struct(shape, f32) for shape in outs] + [struct((devices, 8, LANES), f32)],
        [],
        4,
        *blocks,
        *weights,
        known,
        after=after,
    )


def take_step(plan, sums, place, weights, updates):
    n_exp = plan.n_exp
    n_norms = 4 + 2 * n_exp
    count = len(weights)

    def kernel(place_ref, sums_ref, *refs):
        weight_refs, update_refs = refs[:count], refs[count : 2 * count]
        norm_ref, ratio_ref, new_refs = refs[2 * count], refs[2 * count + 1], refs[2 * count + 2 :]
        total = jnp.sum(sums_ref[...], axis=0)
        lane = lax.broadcasted_iota(jnp.int32, total.shape, 1)
        norms = jnp.sqrt(total)
        norm_ref[...] = norms

        def at(values, index):
            return jnp.sum(jnp.where(lane == index, values, 0.0), axis=1, keepdims=True)

        ratios = jnp.where(lane < 2 * n_norms, 0.0, total)
        for index in range(n_norms):
            ratio = at(norms, 2 * index) / at(norms, 2 * index + 1)
            ratios = jnp.where(lane == 2 * index, ratio, ratios)
        ratio_ref[...] = ratios
        own = place_ref[0]
        rates = [at(ratios, 0), at(ratios, 2), None, at(ratios, 8 + 2 * own)]
        rates.append(at(ratios, 8 + 2 * (n_exp + own)))
        for index in range(count):
            update = update_refs[index][...]
            if index == 2:
                first = lax.broadcasted_iota(jnp.int32, update.shape, 1) == 0
                rate = jnp.where(first, at(ratios, 4)[0:1], at(ratios, 6)[0:1])
            else:
                rate = rates[index][0:1]
            new_refs[index][...] = weight_refs[index][...] - learn_rate * rate * update

    row = struct((8, LANES), f32)
    shapes = [weight.shape for weight in weights]
    return run_kernel(
        kernel,
        (1,),
        [scalars, whole(sums.shape)] + [whole(shape) for shape in shapes] * 2,
        [whole(row.shape)] * 2 + [whole(shape) for shape in shapes],
        [row, row] + [struct(shape, f32) for shape in shapes],
        [],
        5,
        place,
        sums,
        *weights,
        *updates,
    )


def body(
    tokens,
    cotangent,
    lengths,
    routes,
    gate_weights,
    norm_gains,
    gains_first,
    gains_second,
    input_weight,
    input_first,
    input_second,
    output_weight,
    output_first,
    output_second,
    frozen_in,
    frozen_out,
    expert_in,
    inner_first,
    inner_second,
    expert_out,
    outer_first,
    outer_second,
):
    plan = Plan(tokens)
    batch, pos, width = plan.batch, plan.pos, plan.width
    seq_place = lax.axis_index("seq")
    exp_place = lax.axis_index("exp")
    seq_lengths = lengths[0]

    input_rows = input_weight.astype(bf16)
    columns = [
        input_rows[:, part * width + pair * LANES : part * width + (pair + 1) * LANES]
        for chunk in range(plan.chunks)
        for part in range(3)
        for _, pair in plan.held(chunk)
        if pair < plan.pairs
    ]
    gain_rows = jnp.pad(norm_gains.astype(bf16), ((0, 0), (0, LANES - 2)))
    row_weights = jnp.concatenate(columns + [gain_rows, output_weight.astype(bf16)], axis=1)
    row_weights = lax.all_gather(row_weights, "exp", axis=0, tiled=True)
    gains_first_column = 3 * width
    split = gains_first_column + LANES
    weights = lax.all_gather(row_weights[:, :split], "seq", axis=0, tiled=True)
    output_low = lax.all_gather(row_weights[:, split:], "seq", axis=0, tiled=True)
    gains = weights[:, gains_first_column : gains_first_column + 2].astype(f32).T

    positions = seq_place * pos + jnp.arange(pos, dtype=jnp.int32)
    live = (positions[None, :] < seq_lengths[:, None]).astype(jnp.int32).reshape(1, plan.tokens)
    slots, counts = routing(plan, routes.reshape(plan.tokens, 2).T, live)
    gate_columns = gate_weights.reshape(plan.tokens, 2)
    place = exp_place.astype(jnp.int32).reshape(1)
    grads_fixed, grads_train = [
        sent(blocks)
        for blocks in dispatch_grads(
            plan, cotangent.reshape(plan.tokens, width), slots, gate_columns.T, place
        )
    ]

    packed = project(plan, tokens, gains, weights, [grads_train[1], grads_train[3]])
    packed = [over_seq(part.reshape(plan.n_seq, 3, pos, LANES)) for part in packed]
    rows = [lax.rem(seq_place + chunk, batch).astype(jnp.int32) for chunk in range(plan.chunks)]
    units = jnp.stack(rows + [(seq_place // batch).astype(jnp.int32)])
    unit_lengths = [lax.dynamic_slice(seq_lengths, (row,), (1,)) for row in rows]
    attended = []
    for c in range(plan.chunks):
        after = [log for _, log in attended[-1:]]
        if c < 2:
            after.append((grads_train, grads_fixed)[c][2])
        attended.append(attend(plan, packed[c], unit_lengths[c], after))

    def joined(parts):
        if not parts:
            return []
        whole_part = over_seq(jnp.stack([p.reshape(plan.n_seq, pos, LANES) for p in parts], axis=1))
        return [(whole_part, index) for index in range(len(parts))]

    def by_pair(part):
        values, index = part
        return values.reshape((plan.per, batch) + values.shape[1:]), index

    contexts = [context for context, _ in attended]
    earlier = joined(contexts[:-1])
    [ending] = held_until(
        contexts[-1:], [values for values, _ in earlier[:1]] + [grads_fixed[1], grads_fixed[3]]
    )
    contexts = [by_pair(part) for part in earlier + joined([ending])]
    context, middle, second_normed, normed = combine_heads(
        plan, tokens, contexts, gains, output_low
    )

    arrived = packed[-1:] + [log for _, log in attended[:-1]]
    train_blocks, fixed_blocks = held_until(
        [pack_expert(expert_in[0], expert_out[0]), pack_expert(frozen_in[0], frozen_out[0])],
        arrived,
    )
    train_layout = ExpertLayout(plan, lax.all_gather(train_blocks, "seq", axis=0))
    fixed_layout = ExpertLayout(plan, lax.all_gather(fixed_blocks, "seq", axis=0))

    normed_rows = second_normed.reshape(plan.tokens, width)
    train_rows = dispatch(plan, 1, normed_rows, slots, place)
    received_train = sent(train_rows)
    fixed_rows = dispatch(plan, 0, normed_rows, slots, place)
    own_copy, own_result, own_hidden = run_expert(
        plan, True, train_rows[:1], grads_train[:1], train_layout, []
    )
    fixed_rows = held_until(fixed_rows, received_train[1:] + own_copy)
    received_fixed = sent(fixed_rows)
    copy_train, result_train, hidden = run_expert(
        plan, True, received_train[1:], grads_train[1:], train_layout, fixed_rows[:1]
    )
    copy_train, result_train = own_copy + copy_train, own_result + result_train
    returned_train = sent_back(copy_train)
    copy_fixed, result_fixed, _ = run_expert(
        plan, False, received_fixed[1:], grads_fixed[1:], fixed_layout, copy_train[1:2]
    )
    own_copy, own_result, _ = run_expert(
        plan, False, received_fixed[:1], grads_fixed[:1], fixed_layout, copy_fixed[:1]
    )
    copy_fixed, result_fixed = own_copy + copy_fixed, own_result + result_fixed
    returned_fixed = sent_back(copy_fixed)
    expert_local = expert_weight_grads(
        plan,
        received_train,
        grads_train,
        own_hidden + hidden,
        train_layout,
        [copy_fixed[0]] + returned_train[1:],
    )
    normed_all = lax.all_gather(normed, "seq", axis=0)

    turned = slots // plan.cap
    turned = jnp.where(
        slots < 0,
        -1,
        (turned // plan.n_exp) * plan.rows
        + ((turned - exp_place) % plan.n_exp) * plan.cap
        + slots % plan.cap,
    ).T
    middle_grad, output_local, gain_expert_grad, *context_grads = turn_back(
        plan,
        returned_fixed + returned_train,
        turned,
        middle,
        cotangent,
        context,
        gains,
        output_low,
        [expert_local, normed_all],
    )
    output_sums = lax.psum_scatter(output_local, "seq", scatter_dimension=0, tiled=True)
    [expert_local] = held_until([expert_local], [normed_all, gain_expert_grad])
    expert_sums = lax.psum_scatter(expert_local, "seq", scatter_dimension=0, tiled=False)
    results = held_until(result_fixed + result_train, [gain_expert_grad])
    results_fixed, results_train = sent_back(results[: plan.n_exp]), sent_back(results[plan.n_exp :])

    context_grads = joined(context_grads[:1]) + joined(context_grads[1:])
    local_grads, packed_grads = [], []
    for c in range(plan.chunks):
        after = local_grads[-1:] if c else [expert_local] + results[:1]
        if c == 1:
            after += results_train[1:2]
        if c == 2:
            after += [packed_grads[0]] + results_train[1:]
        local_grads.append(
            attend_back(
                plan,
                packed[c],
                attended[c][0],
                context_grads[c],
                attended[c][1],
                unit_lengths[c],
                after,
            )
        )
        if c == 0 and plan.chunks > 1:
            local_grads = held_until(local_grads, [context_grads[1][0]])
        if c < plan.chunks - 1:
            packed_grads.append(over_seq(local_grads[c]))

    late = unit_weight_grads(
        plan,
        local_grads,
        normed_all,
        weights,
        units,
        results_fixed[1:] + [output_sums],
    )
    wide = late.shape[1]
    [late] = held_until([late], packed_grads[1:])
    block_output = mix_results(
        plan, results_fixed + results_train, turned, gate_columns, middle, [late]
    )
    late = over_seq(late.reshape(plan.n_seq, -1, wide))
    packed_grads.append(over_seq(held_until(local_grads[-1:], [late])[0]))
    packed_grads = [part.reshape(plan.per, batch, 3, pos, LANES) for part in packed_grads]
    token_grad = project_back(plan, packed_grads, tokens, gains, weights, middle_grad)
    half = expert_sums.shape[0] // 2
    inner_grad = expert_sums[:half].astype(f32).transpose(1, 0, 2).reshape(expert_in.shape)
    outer_grad = expert_sums[half:].astype(f32).reshape(expert_out.shape)
    inner_moment, inner_square, inner_update = lamb_update(
        expert_in, inner_grad, inner_first, inner_second, decay_rate
    )
    outer_moment, outer_square, outer_update = lamb_update(
        expert_out, outer_grad, outer_first, outer_second, decay_rate
    )
    n_norms = 4 + 2 * plan.n_exp
    picker = (jnp.arange(plan.n_exp, dtype=jnp.int32) == exp_place).astype(f32)[:, None]
    known = jnp.concatenate(
        [
            jnp.zeros((8,), f32),
            (picker * square_pair(expert_in, inner_update)[None]).reshape(-1),
            (picker * square_pair(expert_out, outer_update)[None]).reshape(-1),
            counts[:, 0],
            jnp.zeros((LANES - 2 * n_norms - plan.experts,), f32),
        ]
    )[None]
    own_rows = output_weight.shape[0]
    blocks = fold_rows(
        plan,
        late.reshape(plan.n_seq, plan.n_exp, own_rows, wide),
        output_sums.reshape(plan.n_exp, own_rows, -1),
        place,
        [block_output],
    )
    made = lamb_rows(
        plan,
        sent(blocks),
        [
            input_weight,
            input_first,
            input_second,
            output_weight,
            output_first,
            output_second,
            norm_gains,
            gains_first,
            gains_second,
        ],
        known,
        packed_grads[-1:],
    )
    input_grad, input_moment, input_square, input_update = made[:4]
    output_grad, output_moment, output_square, output_update = made[4:8]
    gains_grad, gains_moment, gains_square, gains_update = made[8:12]
    sums = lax.all_to_all(made[12], ("seq", "exp"), split_axis=0, concat_axis=0, tiled=True)
    norms, ratios, input_new, output_new, gains_new, inner_new, outer_new = take_step(
        plan,
        sums,
        place,
        [input_weight, output_weight, norm_gains, expert_in[0], expert_out[0]],
        [input_update, output_update, gains_update, inner_update[0], outer_update[0]],
    )
    inner_new, outer_new = inner_new[None], outer_new[None]
    matrix_norms = norms[0, : 2 * n_norms].reshape(n_norms, 2)
    trust_ratios = ratios[0, : 2 * n_norms].reshape(n_norms, 2)[:, 0]
    routed_counts = ratios[0, 2 * n_norms : 2 * n_norms + plan.experts].astype(jnp.int32)
    return (
        block_output,
        token_grad,
        gains_grad,
        gains_moment,
        gains_square,
        gains_new,
        input_grad,
        input_moment,
        input_square,
        input_new,
        output_grad,
        output_moment,
        output_square,
        output_new,
        inner_grad,
        inner_moment,
        inner_square,
        inner_new,
        outer_grad,
        outer_moment,
        outer_square,
        outer_new,
        matrix_norms,
        trust_ratios,
        routed_counts,
    )


def solution(mesh):
    tokens_spec, rows_spec = P("exp", "seq", None), P(("seq", "exp"), None)
    return jax.shard_map(
        body,
        mesh=mesh,
        in_specs=(
            (tokens_spec,) * 2
            + (P("exp", None),)
            + (tokens_spec,) * 2
            + (rows_spec,) * 9
            + (tokens_spec,) * 8
        ),
        out_specs=(tokens_spec,) * 2 + (rows_spec,) * 12 + (tokens_spec,) * 8 + (P(),) * 3,
        check_vma=False,
    )
```

time: 1950 us -> 613 us (0.31)
  starting transfers between devices: 517 us -> 111 us
  Pallas kernels: 0 us -> 280 us
  other arithmetic: 293 us -> 22 us
  blocking collectives: 283 us -> 18.8 us
  matrix products: 245 us -> 0 us
  waiting for transfers between devices: 365 us -> 121 us
  local copies, waits for them, and re-layouts: 208 us -> 34 us
    ppermute x32 -> x27, starting transfers between devices: 504 us -> 64.4 us  [shifted(): lax.ppermute(values, 'exp', [(i, (i + distance) % count) for i in range(c...]
    pallas_call x0 -> x34, Pallas kernels: none -> 280 us  [the longest x26 280 us: run_kernel(): pl.pallas_call(run, grid_spec=pltpu.PrefetchScalarGridSpec(num_scalar_pre...]
    dot_general x19 -> x0, matrix products: 245 us -> none  [the longest x1 40.1 us: fold_compute(): jnp.einsum('shqk,skhd->shqd', shifted.astype(jnp.bfloat16), split_heads(v...]
    convert_element_type x44 -> x4, other arithmetic: 133 us -> 2.9 us  [the longest x1 1.26 us: body(): ratios[0, 2 * n_norms:2 * n_norms + plan.experts].astype(jnp.int32)]
    unnamed x1 -> x0, blocking collectives: 100 us -> none
    all_gather x8 -> x5, waiting for transfers between devices: 121 us -> 23.8 us  [the longest x1 22.4 us: body(): weights = lax.all_gather(row_weights[:, :split], 'seq', axis=0, tiled=True)]
    all_to_all x1 -> x0, blocking collectives: 72.7 us -> none  [body(): lax.all_to_all(grad_dispatch, 'exp', split_axis=0, concat_axis=0, tiled=T...]
    reduce_sum x10 -> x0, other arithmetic: 68.2 us -> none  [the longest x1 33.2 us: fold_compute(): new_total = jnp.sum(shifted, axis=-1)]
  transfers between devices with their start and end apart: 47 -> 46, of which waited for: 10 -> 15; matrix products, arithmetic and copies ran while one was open for 34% -> 5% of each run, Pallas kernels for 0% -> 41%
where the time goes in v1:
time: 613 us; the launch traced here: 603 us
  Pallas kernels  280 us (46%)
  waiting for transfers between devices  121 us (20%)
  starting transfers between devices  111 us (18%)
  local copies, waits for them, and re-layouts  34 us (6%)
  other arithmetic  22 us (4%)
  blocking collectives  18.8 us (3%)
  between operations  15.3 us (2%)
    pallas_call x26, Pallas kernels, run_kernel(): pl.pallas_call(run, grid_spec=pltpu.PrefetchScalarGridSpec(num_scalar_pre...  280 us
    all_to_all x11, waiting for transfers between devices, over_seq(): lax.all_to_all(values, 'seq', split_axis=0, concat_axis=0, tiled=True)  82.3 us
    ppermute x27, starting transfers between devices, shifted(): lax.ppermute(values, 'exp', [(i, (i + distance) % count) for i in range(c...  64.4 us
    all_to_all x11, starting transfers between devices, over_seq(): lax.all_to_all(values, 'seq', split_axis=0, concat_axis=0, tiled=True)  43.9 us
    unnamed x131, local copies, waits for them, and re-layouts  25.7 us
    all_gather x1, waiting for transfers between devices, body(): weights = lax.all_gather(row_weights[:, :split], 'seq', axis=0, tiled=True)  22.4 us
    all_gather x1, blocking collectives, body(): row_weights = lax.all_gather(row_weights, 'exp', axis=0, tiled=True)  18.8 us
    ppermute x27, waiting for transfers between devices, shifted(): lax.ppermute(values, 'exp', [(i, (i + distance) % count) for i in range(c...  14 us
  transfers between devices with their start and end apart: 46, of which 15 were waited for; matrix products, arithmetic and copies ran while one was open for 5% of the time, Pallas kernels for 41%

profile of v1, /device:TPU:0, one launch (start us, length us, event | category | flops | bytes accessed | tf_op | source)
XLA Modules:
  0.0 603.4 jit_solution(14051598293609081316)
XLA Ops:
  10.0 18.8 %all_gather.27 = bf16[96,3200]{1,0:T(8,128)(2,1)S(1)} all-gather(bf16[24,3200]{1,0:T(8,128)(2,1)S(1)} %convert_dynamic-update-slice_fusion), channel_id=1, replica_groups=mesh['seq'=8,'exp'=4] {'exp'}, dimensions={0}, use_global_device_ids=true | all-gather | bytes 768000 | tf_op jit(solution)/shard_map/all_gather | solution.py:1170
  33.0 6.1 %shard_map.406 = (bf16[256,768]{1,0:T(8,128)(2,1)}, bf16[256,768]{1,0:T(8,128)(2,1)}, bf16[256,768]{1,0:T(8,128)(2,1)}, bf16[256,768]{1,0:T(8,128)(2,1)}, bf16[2...) custom-call(s32[1]{0:T(128)} %bitcast.7.refs_0_, ...), custom_call_target="tpu_custom_call" | custom-call | flops 9228000256 | tf_op jit(solution)/shard_map/pallas_call | solution.py:51
  43.0 22.4 %all-gather.9.cloned.1.call-done.refs_2_.refs_5_.refs_6_.refs_7_.refs_8_.refs_9_.refs_10_.refs_11_.refs_12_.refs_13_.refs_3_ = bf16[768,2432]{1,0:T(8,128)(2,1)} async-done(((bf16[96,2432]{1,0:T(8,128)(2,1)}), bf16[768,2432]{1,0:T(8,128)(2,1)}) %all-gather.9.cloned.1.call-update) | async-done | bytes 3735568 | tf_op jit(solution)/shard_map/all_gather | solution.py:1173
  68.5 8.2 %shard_map.407 = (bf16[2,4,3,256,128]{4,3,2,1,0:T(8,128)(2,1)}, bf16[2,4,3,256,128]{4,3,2,1,0:T(8,128)(2,1)}, bf16[2,4,3,256,128]{4,3,2,1,0:T(8,128)(2,1)}) custom-call(bf16[4,256,768]{2,1,0:T(8,128)(2,1)} %refs_0_.5, f32[2,768]{1,0:T(2,128)} %copy.143.refs_1_.refs_4_, ...), custom_call_target="tpu_custom_call" | custom-call | flops 9228000256 | tf_op jit(solution)/shard_map/pallas_call | solution.py:51
  76.7 3.7 all-to-all-start
  89.9 13.1 %all-to-all-done.refs_1_ = bf16[8,3,256,128]{3,2,1,0:T(8,128)(2,1)S(1)} async-done(((bf16[8,3,256,128]{3,2,1,0:T(8,128)(2,1)}), bf16[8,3,256,128]{3,2,1,0:T(8,128)(2,1)S(1)}, u32[]{:S(2)}, u32[]{:S(2)}) %all-to-all-start) | async-done | bytes 1572896 | tf_op jit(solution)/shard_map/all_to_all | solution.py:187
  104.1 4.3 all-to-all-start.1
  111.2 17.1 %shard_map.408 = (bf16[8,256,128]{2,1,0:T(8,128)(2,1)}, f32[8,2,256]{2,1,0:T(2,128)}) custom-call(s32[1]{0:T(128)} %bitcast.6.refs_0_, bf16[8,3,256,128]{3,2,1,0:T(8,128)(2,1)} %copy-done.7, bf16[256,768]{1,0:T(8,128)(2,1)} %copy-done.37), custom_call_target="tpu_custom_call" | custom-call | flops 23069999104 | tf_op jit(solution)/shard_map/pallas_call | solution.py:51
  129.4 3.6 all-to-all-start.3
  133.8 12.2 %shard_map.409 = (bf16[8,256,128]{2,1,0:T(8,128)(2,1)}, f32[8,2,256]{2,1,0:T(2,128)}) custom-call(s32[1]{0:T(128)} %bitcast.12.refs_0_, bf16[8,3,256,128]{3,2,1,0:T(8,128)(2,1)} %all-to-all-done.1.refs_1_, f32[8,2,256]{2,1,0:T(2,128)} %get-tuple-element.127.refs_2_.refs_3_.refs_4_, bf16[256,768]{1,0:T(8,128)(2,1)} %copy-done.38), custom_call_target="tpu_custom_call" | custom-call | flops 23069999104 | tf_op jit(solution)/shard_map/pallas_call | solution.py:51
  146.0 8.0 %all-to-all-done.3.refs_1_.refs_2_ = bf16[8,3,256,128]{3,2,1,0:T(8,128)(2,1)S(1)} async-done(((bf16[8,3,256,128]{3,2,1,0:T(8,128)(2,1)}), bf16[8,3,256,128]{3,2,1,0:T(8,128)(2,1)S(1)}, u32[]{:S(2)}, u32[]{:S(2)}) %all-to-all-start.3) | async-done | bytes 1572896 | tf_op jit(solution)/shard_map/all_to_all | solution.py:187
  161.1 3.6 all-to-all-start.2
  164.6 17.6 %shard_map.410 = (bf16[8,256,128]{2,1,0:T(8,128)(2,1)}, f32[8,2,256]{2,1,0:T(2,128)}) custom-call(s32[1]{0:T(128)} %bitcast.16.refs_0_, bf16[8,3,256,128]{3,2,1,0:T(8,128)(2,1)} %copy-done.1, f32[8,2,256]{2,1,0:T(2,128)} %get-tuple-element.131.refs_2_.refs_4_), custom_call_target="tpu_custom_call" | custom-call | flops 23069999104 | tf_op jit(solution)/shard_map/pallas_call | solution.py:51
  184.1 5.8 all-to-all-done.2.refs_1_
  190.9 3.5 all-to-all-start.4
  194.7 14.9 %all-to-all-done.4 = bf16[8,1,256,128]{3,2,1,0:T(8,128)(2,1)S(1)} async-done(((bf16[8,1,256,128]{3,2,1,0:T(8,128)(2,1)}), bf16[8,1,256,128]{3,2,1,0:T(8,128)(2,1)S(1)}, u32[]{:S(2)}, u32[]{:S(2)}) %all-to-all-start.4) | async-done | bytes 524320 | tf_op jit(solution)/shard_map/all_to_all | solution.py:187
  210.4 6.4 %shard_map.412 = (bf16[4,256,768]{2,1,0:T(8,128)(2,1)}, f32[4,256,768]{2,1,0:T(8,128)}, bf16[4,256,768]{2,1,0:T(8,128)(2,1)}, bf16[4,256,768]{2,1,0:T(8,128)(2,1)}) custom-call(bf16[4,256,768]{2,1,0:T(8,128)(2,1)} %refs_0_.5, f32[2,768]{1,0:T(2,128)} %copy.143.refs_1_.refs_4_, bf16[768,768]{1,0:T(8,128)(2,1)} %all-gather.11.cloned.1.call-done.refs_2_.refs_5_, ...), custom_call_target="tpu_custom_call" | custom-call | flops 6920999936 | tf_op jit(solution)/shard_map/pallas_call | solution.py:51
  219.6 4.0 shard_map.414
  228.5 4.1 shard_map.413
  232.6 9.8 %shard_map.418 = (bf16[256,768]{1,0:T(8,128)(2,1)}, bf16[256,768]{1,0:T(8,128)(2,1)}, bf16[256,3072]{1,0:T(8,128)(2,1)}, bf16[256,3072]{1,0:T(8,128)(2,1)}) custom-call(bf16[256,768]{1,0:T(8,128)(2,1)} %get-tuple-element.144.refs_0_, bf16[256,768]{1,0:T(8,128)(2,1)} %get-tuple-element.145.refs_1_.refs_4_, bf16[8,8,96,768]{3,2,1,0:T(8,128)(2,1)} %bitcast.105, ...), custom_call_target="tpu_custom_call" | custom-call | flops 8074500096 | tf_op jit(solution)/shard_map/pallas_call | solution.py:51
  242.4 8.2 %collective-permute-done.7.refs_5_.refs_1_.refs_2_ = bf16[256,768]{1,0:T(8,128)(2,1)S(1)} collective-permute-done((bf16[256,768]{1,0:T(8,128)(2,1)}, bf16[256,768]{1,0:T(8,128)(2,1)S(1)}, u32[]{:S(2)}, u32[]{:S(2)}) %collective-permute-start.7) | collective-permute-done | bytes 393248 | tf_op jit(solution)/shard_map/ppermute | solution.py:200
  251.5 7.2 %collective-permute-start.10 = (bf16[256,768]{1,0:T(8,128)(2,1)}, bf16[256,768]{1,0:T(8,128)(2,1)S(1)}, u32[]{:S(2)}, u32[]{:S(2)}) collective-permute-start(bf16[256,768]{1,0:T(8,128)(2,1)} %get-tuple-element.152), channel_id=1, source_target_pairs={{0,2},{1,3},{2,0},{3,1},{4,6},{5,7},{6,4},{7,5},{8,10},{9,11},{10,... | collective-permute-start | bytes 1179656 | tf_op jit(solution)/shard_map/ppermute | solution.py:200
  262.0 23.1 %shard_map.420 = (bf16[256,768]{1,0:T(8,128)(2,1)}, bf16[256,768]{1,0:T(8,128)(2,1)}, bf16[256,768]{1,0:T(8,128)(2,1)}, bf16[256,768]{1,0:T(8,128)(2,1)}, bf16[2...) custom-call(bf16[256,768]{1,0:T(8,128)(2,1)} %copy-done.19, ...), custom_call_target="tpu_custom_call" | custom-call | flops 24223500288 | tf_op jit(solution)/shard_map/pallas_call | solution.py:51
  285.0 3.8 collective-permute-start.15
  292.1 21.5 %shard_map.421 = (bf16[256,768]{1,0:T(8,128)(2,1)}, bf16[256,768]{1,0:T(8,128)(2,1)}, bf16[256,768]{1,0:T(8,128)(2,1)}, bf16[256,768]{1,0:T(8,128)(2,1)}, bf16[2...) custom-call(bf16[256,768]{1,0:T(8,128)(2,1)} %copy-done.51, bf16[256,768]{1,0:T(8,128)(2,1)} %copy-done.48, ...), custom_call_target="tpu_custom_call" | custom-call | flops 24223500288 | tf_op jit(solution)/shard_map/pallas_call | solution.py:51
  316.9 18.0 %collective-permute-start.13 = (bf16[256,768]{1,0:T(8,128)(2,1)}, bf16[256,768]{1,0:T(8,128)(2,1)S(1)}, u32[]{:S(2)}, u32[]{:S(2)}) collective-permute-start(bf16[256,768]{1,0:T(8,128)(2,1)} %get-tuple-element.166), channel_id=1, source_target_pairs={{0,2},{1,3},{2,0},{3,1},{4,6},{5,7},{6,4},{7,5},{8,10},{9,11},{10,... | collective-permute-start | bytes 1179656 | tf_op jit(solution)/shard_map/ppermute | solution.py:200
  334.9 9.0 %shard_map.422 = (bf16[256,768]{1,0:T(8,128)(2,1)}, bf16[256,768]{1,0:T(8,128)(2,1)}) custom-call(bf16[256,768]{1,0:T(8,128)(2,1)} %get-tuple-element.148.refs_8_.refs_0_, bf16[256,768]{1,0:T(8,128)(2,1)} %get-tuple-element.149.refs_1_, bf16[8,8,96,768]{3,2,1,0:T(8,128)(2,1)} %bitcast.103, bf16[8,8,96,768]{3,2,1,0:T(8,128)(2,1)} %bitcast.104, ...), custom_call_target="tpu_custom_call" | custom-call | flops 8074500096 | tf_op jit(solution)/shard_map/pallas_call | solution.py:51
  346.8 18.4 %shard_map.423.refs_14_.refs_0_ = bf16[8,8,96,768]{3,2,1,0:T(8,128)(2,1)} custom-call(bf16[256,768]{1,0:T(8,128)(2,1)} %get-tuple-element.144.refs_0_, bf16[256,768]{1,0:T(8,128)(2,1)} %copy-done.19, bf16[256,768]{1,0:T(8,128)(2,1)} %copy-done.20, bf16[256,768]{1,0:T(8,128)(2,1)} %copy-done.21, bf16[256,768]{1,0:T(8,128)(2,1)} %get-tuple-element.145.refs_1_.refs_4_, ...), custom_call_target="tpu_custom_call" | custom-call | flops 18456000512 | tf_op jit(solution)/shard_map/pallas_call | solution.py:51
  365.2 3.7 collective-permute-done.13.refs_8_
  369.9 14.8 %shard_map.424 = (f32[4,256,768]{2,1,0:T(8,128)}, bf16[768,896]{1,0:T(8,128)(2,1)}, f32[1,768]{1,0:T(1,128)}, bf16[2,4,256,128]{3,2,1,0:T(8,128)(2,1)}, bf16[2,4...) custom-call(s32[1024,2]{1,0:T(8,128)} %fusion.7.refs_0_, f32[4,256,768]{2,1,0:T(8,128)} %get-tuple-element.135.refs_1_.refs_2_, ...), custom_call_target="tpu_custom_call" | custom-call | flops 13841999872 | tf_op jit(solution)/shard_map/pallas_call | solution.py:51
  385.4 4.4 all-to-all-start.5
  399.6 3.6 all-to-all-start.6
  403.1 20.8 %shard_map.427.refs_0_ = bf16[8,3,256,128]{3,2,1,0:T(8,128)(2,1)} custom-call(s32[1]{0:T(128)} %bitcast.6.refs_0_, bf16[8,3,256,128]{3,2,1,0:T(8,128)(2,1)} %copy-done.7, bf16[8,256,128]{2,1,0:T(8,128)(2,1)} %get-tuple-element.125.refs_2_, bf16[8,1,256,128]{3,2,1,0:T(8,128)(2,1)} %copy-done.12, f32[8,2,256]{2,1,0:T(2,128)} %get-tuple-element.127.refs_2_.refs_3_.refs_4_, ...), custom_call_target="tpu_custom_call" | custom-call | flops 25376999424 | tf_op jit(solution)/shard_map/pallas_call | solution.py:51
  424.9 4.9 all-to-all-start.7
  429.9 14.8 %shard_map.429.refs_5_.refs_2_ = bf16[8,3,256,128]{3,2,1,0:T(8,128)(2,1)} custom-call(s32[1]{0:T(128)} %bitcast.12.refs_0_, bf16[8,3,256,128]{3,2,1,0:T(8,128)(2,1)} %all-to-all-done.1.refs_1_, bf16[8,256,128]{2,1,0:T(8,128)(2,1)} %get-tuple-element.129.refs_2_, bf16[8,2,256,128]{3,2,1,0:T(8,128)(2,1)} %copy-done.4, ...), custom_call_target="tpu_custom_call" | custom-call | flops 25376999424 | tf_op jit(solution)/shard_map/pallas_call | solution.py:51
  444.8 6.1 %all-to-all-done.7.refs_6_ = bf16[8,3,256,128]{3,2,1,0:T(8,128)(2,1)S(1)} async-done(((bf16[8,3,256,128]{3,2,1,0:T(8,128)(2,1)}), bf16[8,3,256,128]{3,2,1,0:T(8,128)(2,1)S(1)}, u32[]{:S(2)}, u32[]{:S(2)}) %all-to-all-start.7) | async-done | bytes 1572896 | tf_op jit(solution)/shard_map/all_to_all | solution.py:187
  452.1 4.1 all-to-all-start.8
  456.3 22.1 %shard_map.430.refs_3_.refs_0_ = bf16[8,3,256,128]{3,2,1,0:T(8,128)(2,1)} custom-call(s32[1]{0:T(128)} %bitcast.16.refs_0_, bf16[8,3,256,128]{3,2,1,0:T(8,128)(2,1)} %copy-done.1, bf16[8,256,128]{2,1,0:T(8,128)(2,1)} %get-tuple-element.132.refs_2_, bf16[8,2,256,128]{3,2,1,0:T(8,128)(2,1)} %copy-done.4, f32[8,2,256]{2,1,0:T(2,128)} %get-tuple-element.187.refs_4_, ...), custom_call_target="tpu_custom_call" | custom-call | flops 25376999424 | tf_op jit(solution)/shard_map/pallas_call | solution.py:51
  478.5 13.4 %shard_map.431.refs_0_ = bf16[768,1280]{1,0:T(8,128)(2,1)} custom-call(s32[4]{0:T(128)} %pad_add_fusion.refs_0_, bf16[8,3,256,128]{3,2,1,0:T(8,128)(2,1)} %shard_map.428.refs_5_.refs_1_, bf16[8,3,256,128]{3,2,1,0:T(8,128)(2,1)} %shard_map.429.refs_5_.refs_2_, bf16[8,3,256,128]{3,2,1,0:T(8,128)(2,1)} %shard_map.430.refs_3_.refs_0_, ...), custom_call_target="tpu_custom_call" | custom-call | flops 14995500032 | tf_op jit(solution)/shard_map/pallas_call | solution.py:51
  495.2 3.7 all-to-all-start.9
  501.1 10.8 %shard_map.433.refs_3_ = bf16[4,256,768]{2,1,0:T(8,128)(2,1)} custom-call(s32[1024,2]{1,0:T(8,128)} %fusion.7.refs_0_, f32[1024,2]{1,0:T(8,128)} %bitcast.83, f32[4,256,768]{2,1,0:T(8,128)} %get-tuple-element.135.refs_1_.refs_2_, bf16[256,768]{1,0:T(8,128)(2,1)} %get-tuple-element.176.refs_6_.refs_3_, ...), custom_call_target="tpu_custom_call" | custom-call | flops 11534999552 | tf_op jit(solution)/shard_map/pallas_call | solution.py:51
  511.9 21.8 %all-to-all-done.9.refs_1_ = bf16[8,96,1280]{2,1,0:T(8,128)(2,1)S(1)} async-done(((bf16[8,96,1280]{2,1,0:T(8,128)(2,1)}), bf16[8,96,1280]{2,1,0:T(8,128)(2,1)S(1)}, u32[]{:S(2)}, u32[]{:S(2)}) %all-to-all-start.9) | async-done | bytes 1966112 | tf_op jit(solution)/shard_map/all_to_all | solution.py:187
  538.3 4.5 collective-permute-start.25
  542.8 4.5 all-to-all-start.10
  550.2 5.5 multiply_reduce_fusion
  562.3 6.1 %all-to-all-done.10 = bf16[8,3,256,128]{3,2,1,0:T(8,128)(2,1)} async-done(((bf16[8,3,256,128]{3,2,1,0:T(8,128)(2,1)}), bf16[8,3,256,128]{3,2,1,0:T(8,128)(2,1)}, u32[]{:S(2)}, u32[]{:S(2)}) %all-to-all-start.10) | async-done | bytes 1572896 | tf_op jit(solution)/shard_map/all_to_all | solution.py:187
  573.8 9.8 %shard_map.435 = f32[4,256,768]{2,1,0:T(8,128)} custom-call(bf16[4,256,768]{2,1,0:T(8,128)(2,1)} %refs_0_.5, f32[2,768]{1,0:T(2,128)} %copy.143.refs_1_.refs_4_, f32[4,256,768]{2,1,0:T(8,128)} %get-tuple-element.189.refs_2_, ...), custom_call_target="tpu_custom_call" | custom-call | flops 11534999552 | tf_op jit(solution)/shard_map/pallas_call | solution.py:51
  586.2 4.5 shard_map.438
  (254 shorter events, 108.1 us)
Async XLA Ops:
  7.2 58.1 %all-gather.9.cloned.1.call-start = ((), (), s32[]{:S(2)}) async-start(), calls=%async_computation.14 | async-start | bytes 4202496 | tf_op jit(solution)/shard_map/all_gather | solution.py:1173
  8.3 21.3 %copy-start.30 = (s32[1,4]{1,0:T(1,128)S(1)}, s32[1,4]{1,0:T(1,128)}, u32[]{:S(2)}) copy-start(s32[1,4]{1,0:T(1,128)} %param.24) | copy-start | bytes 52
  8.3 22.0 %copy-start.28 = (f32[4,256,2]{1,2,0:T(2,128)S(1)}, f32[4,256,2]{1,2,0:T(2,128)}, u32[]{:S(2)}) copy-start(f32[4,256,2]{1,2,0:T(2,128)} %param.26) | copy-start | bytes 24580
  39.1 27.9 %collective-permute-start = (bf16[256,768]{1,0:T(8,128)(2,1)}, bf16[256,768]{1,0:T(8,128)(2,1)S(1)}, u32[]{:S(2)}, u32[]{:S(2)}) collective-permute-start(bf16[256,768]{1,0:T(8,128)(2,1)} %get-tuple-element.121), channel_id=1, source_target_pairs={{0,1},{1,2},{2,3},{3,0},{4,5},{5,6},{6,7},{7,4},{8,9},{9,10},{10,1... | collective-permute-start | bytes 1179656 | tf_op jit(solution)/shard_map/ppermute | solution.py:200
  40.3 26.8 %collective-permute-start.1 = (bf16[256,768]{1,0:T(8,128)(2,1)}, bf16[256,768]{1,0:T(8,128)(2,1)S(1)}, u32[]{:S(2)}, u32[]{:S(2)}) collective-permute-start(bf16[256,768]{1,0:T(8,128)(2,1)} %get-tuple-element.122), channel_id=1, source_target_pairs={{0,3},{1,0},{2,1},{3,2},{4,7},{5,4},{6,5},{7,6},{8,11},{9,8},{10,9... | collective-permute-start | bytes 1179656 | tf_op jit(solution)/shard_map/ppermute | solution.py:200
  76.7 26.3 %all-to-all-start = ((bf16[8,3,256,128]{3,2,1,0:T(8,128)(2,1)}), bf16[8,3,256,128]{3,2,1,0:T(8,128)(2,1)S(1)}, u32[]{:S(2)}, u32[]{:S(2)}) async-start(bf16[8,3,256,128]{3,2,1,0:T(8,128)(2,1)} %bitcast.86), calls=%async_computation | async-start | bytes 3145728 | tf_op jit(solution)/shard_map/all_to_all | solution.py:187
  80.4 114.3 %all-gather.11.cloned.1.call-start = ((), (), s32[]{:S(2)}) async-start(), calls=%async_computation.15 | async-start | bytes 1327104 | tf_op jit(solution)/shard_map/all_gather | solution.py:1174
  80.5 30.0 %collective-permute-start.2 = (bf16[256,768]{1,0:T(8,128)(2,1)}, bf16[256,768]{1,0:T(8,128)(2,1)S(1)}, u32[]{:S(2)}, u32[]{:S(2)}) collective-permute-start(bf16[256,768]{1,0:T(8,128)(2,1)} %get-tuple-element.124), channel_id=1, source_target_pairs={{0,2},{1,3},{2,0},{3,1},{4,6},{5,7},{6,4},{7,5},{8,10},{9,11},{10,... | collective-permute-start | bytes 1179656 | tf_op jit(solution)/shard_map/ppermute | solution.py:200
  82.9 50.1 %collective-permute-start.3 = (bf16[256,768]{1,0:T(8,128)(2,1)S(1)}, bf16[256,768]{1,0:T(8,128)(2,1)S(1)}, u32[]{:S(2)}, u32[]{:S(2)}) collective-permute-start(bf16[256,768]{1,0:T(8,128)(2,1)S(1)} %copy-done.41), channel_id=1, source_target_pairs={{0,2},{1,3},{2,0},{3,1},{4,6},{5,7},{6,4},{7,5},{8,10},{9,11},{10,... | collective-permute-start | bytes 1179656 | tf_op jit(solution)/shard_map/ppermute | solution.py:200
  104.1 25.3 %all-to-all-start.1 = ((bf16[8,3,256,128]{3,2,1,0:T(8,128)(2,1)}), bf16[8,3,256,128]{3,2,1,0:T(8,128)(2,1)}, u32[]{:S(2)}, u32[]{:S(2)}) async-start(bf16[8,3,256,128]{3,2,1,0:T(8,128)(2,1)} %bitcast.85), calls=%async_computation.1 | async-start | bytes 3145728 | tf_op jit(solution)/shard_map/all_to_all | solution.py:187
  129.4 24.5 %all-to-all-start.3 = ((bf16[8,3,256,128]{3,2,1,0:T(8,128)(2,1)}), bf16[8,3,256,128]{3,2,1,0:T(8,128)(2,1)S(1)}, u32[]{:S(2)}, u32[]{:S(2)}) async-start(bf16[8,3,256,128]{3,2,1,0:T(8,128)(2,1)} %bitcast.17), calls=%async_computation.3 | async-start | bytes 3145728 | tf_op jit(solution)/shard_map/all_to_all | solution.py:187
  133.0 99.5 %all-gather.13.cloned.1.call-start = ((), (), s32[]{:S(2)}) async-start(), calls=%async_computation.18 | async-start | bytes 10616832 | tf_op jit(solution)/shard_map/all_gather | solution.py:1226
  155.2 136.0 %all-gather.15.cloned.1.call-start = ((), (), s32[]{:S(2)}) async-start(), calls=%async_computation.19 | async-start | bytes 10616832 | tf_op jit(solution)/shard_map/all_gather | solution.py:1227
  156.2 27.9 %collective-permute-start.4 = (bf16[256,768]{1,0:T(8,128)(2,1)S(1)}, bf16[256,768]{1,0:T(8,128)(2,1)S(1)}, u32[]{:S(2)}, u32[]{:S(2)}) collective-permute-start(bf16[256,768]{1,0:T(8,128)(2,1)S(1)} %copy-done.40), channel_id=1, source_target_pairs={{0,1},{1,2},{2,3},{3,0},{4,5},{5,6},{6,7},{7,4},{8,9},{9,10},{10,1... | collective-permute-start | bytes 1179656 | tf_op jit(solution)/shard_map/ppermute | solution.py:200
  157.7 26.4 %collective-permute-start.5 = (bf16[256,768]{1,0:T(8,128)(2,1)S(1)}, bf16[256,768]{1,0:T(8,128)(2,1)S(1)}, u32[]{:S(2)}, u32[]{:S(2)}) collective-permute-start(bf16[256,768]{1,0:T(8,128)(2,1)S(1)} %copy-done.39), channel_id=1, source_target_pairs={{0,3},{1,0},{2,1},{3,2},{4,7},{5,4},{6,5},{7,6},{8,11},{9,8},{10,9... | collective-permute-start | bytes 1179656 | tf_op jit(solution)/shard_map/ppermute | solution.py:200
  161.1 28.8 %all-to-all-start.2 = ((bf16[8,2,256,128]{3,2,1,0:T(8,128)(2,1)}), bf16[8,2,256,128]{3,2,1,0:T(8,128)(2,1)S(1)}, u32[]{:S(2)}, u32[]{:S(2)}) async-start(bf16[8,2,256,128]{3,2,1,0:T(8,128)(2,1)} %pad_maximum_fusion), calls=%async_computation.2 | async-start | bytes 2097152 | tf_op jit(solution)/shard_map/all_to_all | solution.py:187
  190.9 18.7 %all-to-all-start.4 = ((bf16[8,1,256,128]{3,2,1,0:T(8,128)(2,1)}), bf16[8,1,256,128]{3,2,1,0:T(8,128)(2,1)S(1)}, u32[]{:S(2)}, u32[]{:S(2)}) async-start(bf16[8,1,256,128]{3,2,1,0:T(8,128)(2,1)} %bitcast.79), calls=%async_computation.4 | async-start | bytes 1048576 | tf_op jit(solution)/shard_map/all_to_all | solution.py:187
  194.4 174.5 %all-gather.17.cloned.1.call-start = ((), (), s32[]{:S(2)}) async-start(), calls=%async_computation.20 | async-start | bytes 14155776 | tf_op jit(solution)/shard_map/all_gather | solution.py:1259
  216.9 261.6 %reduce-scatter.3.cloned.1.call-start = ((), (), s32[]{:S(2)}) async-start(), calls=%async_computation.16 | async-start | bytes 1548288 | tf_op jit(solution)/shard_map/reduce_scatter | solution.py:1280
  223.5 18.8 %collective-permute-start.6 = (bf16[256,768]{1,0:T(8,128)(2,1)}, bf16[256,768]{1,0:T(8,128)(2,1)S(1)}, u32[]{:S(2)}, u32[]{:S(2)}) collective-permute-start(bf16[256,768]{1,0:T(8,128)(2,1)} %get-tuple-element.141), channel_id=1, source_target_pairs={{0,1},{1,2},{2,3},{3,0},{4,5},{5,6},{6,7},{7,4},{8,9},{9,10},{10,1... | collective-permute-start | bytes 1179656 | tf_op jit(solution)/shard_map/ppermute | solution.py:200
  224.6 26.0 %collective-permute-start.7 = (bf16[256,768]{1,0:T(8,128)(2,1)}, bf16[256,768]{1,0:T(8,128)(2,1)S(1)}, u32[]{:S(2)}, u32[]{:S(2)}) collective-permute-start(bf16[256,768]{1,0:T(8,128)(2,1)} %get-tuple-element.142), channel_id=1, source_target_pairs={{0,2},{1,3},{2,0},{3,1},{4,6},{5,7},{6,4},{7,5},{8,10},{9,11},{10,... | collective-permute-start | bytes 1179656 | tf_op jit(solution)/shard_map/ppermute | solution.py:200
  227.0 23.5 %collective-permute-start.8 = (bf16[256,768]{1,0:T(8,128)(2,1)}, bf16[256,768]{1,0:T(8,128)(2,1)S(1)}, u32[]{:S(2)}, u32[]{:S(2)}) collective-permute-start(bf16[256,768]{1,0:T(8,128)(2,1)} %get-tuple-element.143), channel_id=1, source_target_pairs={{0,3},{1,0},{2,1},{3,2},{4,7},{5,4},{6,5},{7,6},{8,11},{9,8},{10,9... | collective-permute-start | bytes 1179656 | tf_op jit(solution)/shard_map/ppermute | solution.py:200
  251.5 37.3 %collective-permute-start.10 = (bf16[256,768]{1,0:T(8,128)(2,1)}, bf16[256,768]{1,0:T(8,128)(2,1)S(1)}, u32[]{:S(2)}, u32[]{:S(2)}) collective-permute-start(bf16[256,768]{1,0:T(8,128)(2,1)} %get-tuple-element.152), channel_id=1, source_target_pairs={{0,2},{1,3},{2,0},{3,1},{4,6},{5,7},{6,4},{7,5},{8,10},{9,11},{10,... | collective-permute-start | bytes 1179656 | tf_op jit(solution)/shard_map/ppermute | solution.py:200
  258.7 32.5 %collective-permute-start.11 = (bf16[256,768]{1,0:T(8,128)(2,1)}, bf16[256,768]{1,0:T(8,128)(2,1)S(1)}, u32[]{:S(2)}, u32[]{:S(2)}) collective-permute-start(bf16[256,768]{1,0:T(8,128)(2,1)} %get-tuple-element.153), channel_id=1, source_target_pairs={{0,3},{1,0},{2,1},{3,2},{4,7},{5,4},{6,5},{7,6},{8,11},{9,8},{10,9... | collective-permute-start | bytes 1179656 | tf_op jit(solution)/shard_map/ppermute | solution.py:200
  262.0 29.3 %collective-permute-start.9 = (bf16[256,768]{1,0:T(8,128)(2,1)}, bf16[256,768]{1,0:T(8,128)(2,1)S(1)}, u32[]{:S(2)}, u32[]{:S(2)}) collective-permute-start(bf16[256,768]{1,0:T(8,128)(2,1)} %get-tuple-element.151), channel_id=1, source_target_pairs={{0,1},{1,2},{2,3},{3,0},{4,5},{5,6},{6,7},{7,4},{8,9},{9,10},{10,1... | collective-permute-start | bytes 1179656 | tf_op jit(solution)/shard_map/ppermute | solution.py:200
  285.0 58.9 %collective-permute-start.15 = (bf16[256,768]{1,0:T(8,128)(2,1)}, bf16[256,768]{1,0:T(8,128)(2,1)S(1)}, u32[]{:S(2)}, u32[]{:S(2)}) collective-permute-start(bf16[256,768]{1,0:T(8,128)(2,1)} %get-tuple-element.154.refs_8_), channel_id=1, source_target_pairs={{0,3},{1,0},{2,1},{3,2},{4,7},{5,4},{6,5},{7,6},{8,11},{9,8},{10,9... | collective-permute-start | bytes 1179656 | tf_op jit(solution)/shard_map/ppermute | solution.py:200
  288.8 57.1 %collective-permute-start.16 = (bf16[256,768]{1,0:T(8,128)(2,1)}, bf16[256,768]{1,0:T(8,128)(2,1)S(1)}, u32[]{:S(2)}, u32[]{:S(2)}) collective-permute-start(bf16[256,768]{1,0:T(8,128)(2,1)} %get-tuple-element.168), channel_id=1, source_target_pairs={{0,2},{1,3},{2,0},{3,1},{4,6},{5,7},{6,4},{7,5},{8,10},{9,11},{10,... | collective-permute-start | bytes 1179656 | tf_op jit(solution)/shard_map/ppermute | solution.py:200
  288.8 57.1 %collective-permute-start.17 = (bf16[256,768]{1,0:T(8,128)(2,1)}, bf16[256,768]{1,0:T(8,128)(2,1)S(1)}, u32[]{:S(2)}, u32[]{:S(2)}) collective-permute-start(bf16[256,768]{1,0:T(8,128)(2,1)} %get-tuple-element.169), channel_id=1, source_target_pairs={{0,1},{1,2},{2,3},{3,0},{4,5},{5,6},{6,7},{7,4},{8,9},{9,10},{10,1... | collective-permute-start | bytes 1179656 | tf_op jit(solution)/shard_map/ppermute | solution.py:200
  313.6 51.6 %collective-permute-start.12 = (bf16[256,768]{1,0:T(8,128)(2,1)}, bf16[256,768]{1,0:T(8,128)(2,1)S(1)}, u32[]{:S(2)}, u32[]{:S(2)}) collective-permute-start(bf16[256,768]{1,0:T(8,128)(2,1)} %get-tuple-element.155.refs_4_), channel_id=1, source_target_pairs={{0,3},{1,0},{2,1},{3,2},{4,7},{5,4},{6,5},{7,6},{8,11},{9,8},{10,9... | collective-permute-start | bytes 1179656 | tf_op jit(solution)/shard_map/ppermute | solution.py:200
  316.9 52.0 %collective-permute-start.13 = (bf16[256,768]{1,0:T(8,128)(2,1)}, bf16[256,768]{1,0:T(8,128)(2,1)S(1)}, u32[]{:S(2)}, u32[]{:S(2)}) collective-permute-start(bf16[256,768]{1,0:T(8,128)(2,1)} %get-tuple-element.166), channel_id=1, source_target_pairs={{0,2},{1,3},{2,0},{3,1},{4,6},{5,7},{6,4},{7,5},{8,10},{9,11},{10,... | collective-permute-start | bytes 1179656 | tf_op jit(solution)/shard_map/ppermute | solution.py:200
  343.9 25.0 %collective-permute-start.14 = (bf16[256,768]{1,0:T(8,128)(2,1)S(1)}, bf16[256,768]{1,0:T(8,128)(2,1)S(1)}, u32[]{:S(2)}, u32[]{:S(2)}) collective-permute-start(bf16[256,768]{1,0:T(8,128)(2,1)S(1)} %copy-done.47), channel_id=1, source_target_pairs={{0,1},{1,2},{2,3},{3,0},{4,5},{5,6},{6,7},{7,4},{8,9},{9,10},{10,1... | collective-permute-start | bytes 1179656 | tf_op jit(solution)/shard_map/ppermute | solution.py:200
  384.7 162.7 %reduce-scatter.5.cloned.1.call-start = ((), (), s32[]{:S(2)}) async-start(), calls=%async_computation.17 | async-start | bytes 10616832 | tf_op jit(solution)/shard_map/reduce_scatter | solution.py:1282
  385.4 14.1 %all-to-all-start.5 = ((bf16[8,1,256,128]{3,2,1,0:T(8,128)(2,1)}), bf16[8,1,256,128]{3,2,1,0:T(8,128)(2,1)S(1)}, u32[]{:S(2)}, u32[]{:S(2)}) async-start(bf16[8,1,256,128]{3,2,1,0:T(8,128)(2,1)} %bitcast.33), calls=%async_computation.5 | async-start | bytes 1048576 | tf_op jit(solution)/shard_map/all_to_all | solution.py:187
  390.4 39.5 %collective-permute-start.21 = (bf16[256,768]{1,0:T(8,128)(2,1)}, bf16[256,768]{1,0:T(8,128)(2,1)}, u32[]{:S(2)}, u32[]{:S(2)}) collective-permute-start(bf16[256,768]{1,0:T(8,128)(2,1)} %get-tuple-element.181), channel_id=1, source_target_pairs={{0,3},{1,0},{2,1},{3,2},{4,7},{5,4},{6,5},{7,6},{8,11},{9,8},{10,9... | collective-permute-start | bytes 1179656 | tf_op jit(solution)/shard_map/ppermute | solution.py:200
  390.4 65.8 %collective-permute-start.22 = (bf16[256,768]{1,0:T(8,128)(2,1)}, bf16[256,768]{1,0:T(8,128)(2,1)}, u32[]{:S(2)}, u32[]{:S(2)}) collective-permute-start(bf16[256,768]{1,0:T(8,128)(2,1)} %get-tuple-element.182), channel_id=1, source_target_pairs={{0,2},{1,3},{2,0},{3,1},{4,6},{5,7},{6,4},{7,5},{8,10},{9,11},{10,... | collective-permute-start | bytes 1179656 | tf_op jit(solution)/shard_map/ppermute | solution.py:200
  390.5 65.8 %collective-permute-start.23 = (bf16[256,768]{1,0:T(8,128)(2,1)}, bf16[256,768]{1,0:T(8,128)(2,1)}, u32[]{:S(2)}, u32[]{:S(2)}) collective-permute-start(bf16[256,768]{1,0:T(8,128)(2,1)} %get-tuple-element.183), channel_id=1, source_target_pairs={{0,1},{1,2},{2,3},{3,0},{4,5},{5,6},{6,7},{7,4},{8,9},{9,10},{10,1... | collective-permute-start | bytes 1179656 | tf_op jit(solution)/shard_map/ppermute | solution.py:200
  392.4 86.0 %collective-permute-start.18 = (bf16[256,768]{1,0:T(8,128)(2,1)}, bf16[256,768]{1,0:T(8,128)(2,1)}, u32[]{:S(2)}, u32[]{:S(2)}) collective-permute-start(bf16[256,768]{1,0:T(8,128)(2,1)} %get-tuple-element.177), channel_id=1, source_target_pairs={{0,3},{1,0},{2,1},{3,2},{4,7},{5,4},{6,5},{7,6},{8,11},{9,8},{10,9... | collective-permute-start | bytes 1179656 | tf_op jit(solution)/shard_map/ppermute | solution.py:200
  394.8 83.6 %collective-permute-start.19 = (bf16[256,768]{1,0:T(8,128)(2,1)}, bf16[256,768]{1,0:T(8,128)(2,1)}, u32[]{:S(2)}, u32[]{:S(2)}) collective-permute-start(bf16[256,768]{1,0:T(8,128)(2,1)} %get-tuple-element.178), channel_id=1, source_target_pairs={{0,2},{1,3},{2,0},{3,1},{4,6},{5,7},{6,4},{7,5},{8,10},{9,11},{10,... | collective-permute-start | bytes 1179656 | tf_op jit(solution)/shard_map/ppermute | solution.py:200
  399.6 24.4 %all-to-all-start.6 = ((bf16[8,2,256,128]{3,2,1,0:T(8,128)(2,1)}), bf16[8,2,256,128]{3,2,1,0:T(8,128)(2,1)S(1)}, u32[]{:S(2)}, u32[]{:S(2)}) async-start(bf16[8,2,256,128]{3,2,1,0:T(8,128)(2,1)} %pad_maximum_fusion.1), calls=%async_computation.6 | async-start | bytes 2097152 | tf_op jit(solution)/shard_map/all_to_all | solution.py:187
  424.9 25.9 %all-to-all-start.7 = ((bf16[8,3,256,128]{3,2,1,0:T(8,128)(2,1)}), bf16[8,3,256,128]{3,2,1,0:T(8,128)(2,1)S(1)}, u32[]{:S(2)}, u32[]{:S(2)}) async-start(bf16[8,3,256,128]{3,2,1,0:T(8,128)(2,1)} %shard_map.428.refs_5_.refs_1_), calls=%async_computation.7 | async-start | bytes 3145728 | tf_op jit(solution)/shard_map/all_to_all | solution.py:187
  429.9 48.5 %collective-permute-start.20 = (bf16[256,768]{1,0:T(8,128)(2,1)S(1)}, bf16[256,768]{1,0:T(8,128)(2,1)}, u32[]{:S(2)}, u32[]{:S(2)}) collective-permute-start(bf16[256,768]{1,0:T(8,128)(2,1)S(1)} %copy-done.18), channel_id=1, source_target_pairs={{0,1},{1,2},{2,3},{3,0},{4,5},{5,6},{6,7},{7,4},{8,9},{9,10},{10,1... | collective-permute-start | bytes 1179656 | tf_op jit(solution)/shard_map/ppermute | solution.py:200
  452.1 41.9 %all-to-all-start.8 = ((bf16[8,3,256,128]{3,2,1,0:T(8,128)(2,1)}), bf16[8,3,256,128]{3,2,1,0:T(8,128)(2,1)S(1)}, u32[]{:S(2)}, u32[]{:S(2)}) async-start(bf16[8,3,256,128]{3,2,1,0:T(8,128)(2,1)} %shard_map.429.refs_5_.refs_2_), calls=%async_computation.9 | async-start | bytes 3145728 | tf_op jit(solution)/shard_map/all_to_all | solution.py:187
  495.2 38.5 %all-to-all-start.9 = ((bf16[8,96,1280]{2,1,0:T(8,128)(2,1)}), bf16[8,96,1280]{2,1,0:T(8,128)(2,1)S(1)}, u32[]{:S(2)}, u32[]{:S(2)}) async-start(bf16[8,96,1280]{2,1,0:T(8,128)(2,1)} %bitcast.77), calls=%async_computation.10 | async-start | bytes 3932160 | tf_op jit(solution)/shard_map/all_to_all | solution.py:187
  537.5 24.8 %collective-permute-start.24 = (bf16[24,3456]{1,0:T(8,128)(2,1)}, bf16[24,3456]{1,0:T(8,128)(2,1)S(1)}, u32[]{:S(2)}, u32[]{:S(2)}) collective-permute-start(bf16[24,3456]{1,0:T(8,128)(2,1)} %get-tuple-element.191), channel_id=1, source_target_pairs={{0,1},{1,2},{2,3},{3,0},{4,5},{5,6},{6,7},{7,4},{8,9},{9,10},{10,1... | collective-permute-start | bytes 497672 | tf_op jit(solution)/shard_map/ppermute | solution.py:200
  538.3 24.0 %collective-permute-start.25 = (bf16[24,3456]{1,0:T(8,128)(2,1)}, bf16[24,3456]{1,0:T(8,128)(2,1)S(1)}, u32[]{:S(2)}, u32[]{:S(2)}) collective-permute-start(bf16[24,3456]{1,0:T(8,128)(2,1)} %get-tuple-element.192), channel_id=1, source_target_pairs={{0,2},{1,3},{2,0},{3,1},{4,6},{5,7},{6,4},{7,5},{8,10},{9,11},{10,... | collective-permute-start | bytes 497672 | tf_op jit(solution)/shard_map/ppermute | solution.py:200
  542.8 19.5 %collective-permute-start.26 = (bf16[24,3456]{1,0:T(8,128)(2,1)}, bf16[24,3456]{1,0:T(8,128)(2,1)S(1)}, u32[]{:S(2)}, u32[]{:S(2)}) collective-permute-start(bf16[24,3456]{1,0:T(8,128)(2,1)} %get-tuple-element.193), channel_id=1, source_target_pairs={{0,3},{1,0},{2,1},{3,2},{4,7},{5,4},{6,5},{7,6},{8,11},{9,8},{10,9... | collective-permute-start | bytes 497672 | tf_op jit(solution)/shard_map/ppermute | solution.py:200
  542.8 25.6 %all-to-all-start.10 = ((bf16[8,3,256,128]{3,2,1,0:T(8,128)(2,1)}), bf16[8,3,256,128]{3,2,1,0:T(8,128)(2,1)}, u32[]{:S(2)}, u32[]{:S(2)}) async-start(bf16[8,3,256,128]{3,2,1,0:T(8,128)(2,1)} %shard_map.434), calls=%async_computation.11 | async-start | bytes 3145728 | tf_op jit(solution)/shard_map/all_to_all | solution.py:187
  571.2 14.4 %all-to-all-start.11 = ((f32[32,8,128]{2,1,0:T(8,128)}), f32[32,8,128]{2,1,0:T(8,128)S(1)}, u32[]{:S(2)}, u32[]{:S(2)}) async-start(f32[32,8,128]{2,1,0:T(8,128)} %get-tuple-element.198), calls=%async_computation.13 | async-start | bytes 262144 | tf_op jit(solution)/shard_map/all_to_all | solution.py:1375
  (53 other events, 188.4 us)
Sparse Core Ops, SparseCore 0:
  29.7 35.5 all-gather.8
  84.3 27.6 all-gather.10
  155.3 74.7 all-gather.12
  232.5 58.6 all-gather.14
  293.0 72.1 all-gather.16
  384.8 42.9 reduce-scatter.2
  431.6 105.7 reduce-scatter.4
